TPU v7x, 128 devices: a whole 4x4x4 slice. The times are simulated.
128 devices in a mesh: dp: 32 (over x, y, core), rep: 4 (over z).
Axes of the slice: x: 4, y: 4, z: 4, core: 2. Of those that a mesh axis runs over, the one named last changes fastest.
Arguments:
- frames: bfloat16 [2048, 4, 16, 4096], P('dp', 'rep'), may hold values from -6 to 6
- clip_lengths: int32 [32, 4, 4], P('dp', 'rep'), may hold values from 1 to 912, as said below
- block_dest: int32 [32, 4, 2, 64], P('dp', 'rep'), may hold values from -1 to 31, as said below
- frame_codes: int32 [2048, 4, 16], P('dp', 'rep'), may hold values from 0 to 1023
- codebook: bfloat16 [1024, 128], replicated, may hold values from -4 to 4
- encoder_weight: bfloat16 [4096, 512], replicated, may hold values from -0.09375 to 0.09375
- latent_weight: bfloat16 [512, 128], replicated, may hold values from -0.25 to 0.25
- expand_weight: bfloat16 [512, 128], replicated, may hold values from -0.5 to 0.5
- decoder_weight: bfloat16 [512, 4096], replicated, may hold values from -0.25 to 0.25
Outputs:
- latents: float32 [1024, 4, 16, 128], P('dp', 'rep')
- grad_encoder: float32 [4096, 512], P(('dp', 'rep'))
- grad_latent: float32 [512, 128], P(('dp', 'rep'))
- grad_expand: float32 [512, 128], P(('dp', 'rep'))
- grad_decoder: float32 [512, 4096], P(('dp', 'rep'))
Inputs may be any that keep to these rules, and one draw needn't show every extreme that they name: `clip_lengths`: each device's clips take ceil(length / 16) slots each; one device uses between 4 and 60 slots, some device of each rep index exactly 60, and the devices of one rep index use 32 slots each on average. `block_dest`: row 0 is the receiving dp index (same rep index), row 1 the receiving slot, both -1 exactly for the slots that no clip uses. Every device receives exactly 32 blocks, one into each slot, and at most 2 blocks from any one device; some device sends 2 blocks to one device.
All inputs are finite; a program needn't handle non-finite values.
Results may differ from a plain program's by a relative error of at most 0.0059.
Values may be sent and summed in bfloat16 or wider, within the bound.
No kernel may reach another device: no remote copies, remote signals or barrier semaphores. Data moves between devices by JAX's collectives and lax.ppermute only.
A program may use at most 128 MiB of HBM per device.

v0:
```python
import jax
import jax.numpy as jnp
from jax import lax
from jax.sharding import PartitionSpec as P

BLK = 16
NB = 64


def elu_slope(values):
    return jnp.where(values > 0, 1.0, jnp.exp(jnp.minimum(values, 0.0)))


def across_rows(left, right):
    return lax.dot_general(
        left, right, (((0,), (0,)), ((), ())), preferred_element_type=jnp.float32
    )


def against_rows(left, right):
    return lax.dot_general(
        left, right, (((1,), (1,)), ((), ())), preferred_element_type=jnp.float32
    )


def row_lengths(lengths):
    blocks = (lengths + BLK - 1) // BLK
    ends = jnp.cumsum(blocks, axis=-1)
    starts = ends - blocks
    position = jnp.arange(NB * BLK, dtype=jnp.int32)
    slot_index = position // BLK
    member = (slot_index >= starts[..., None] * 1) & (slot_index < ends[..., None])
    offset = position - starts[..., None] * BLK
    valid = member & (offset < lengths[..., None])
    counted = jnp.sum(jnp.where(valid, lengths[..., None], 0), axis=-2)
    return counted.reshape(lengths.shape[:-1] + (NB, BLK))


def train_rows(
    placed,
    row_codes,
    row_length,
    codebook,
    encoder_weight,
    latent_weight,
    expand_weight,
    decoder_weight,
    reduce_decoder,
):
    pre_hidden = jnp.dot(placed, encoder_weight, preferred_element_type=jnp.float32)
    hidden = jax.nn.elu(pre_hidden).astype(jnp.bfloat16)
    latents = jnp.dot(hidden, latent_weight, preferred_element_type=jnp.float32)
    quantized = jnp.take(codebook, row_codes, axis=0)
    pre_decoded = against_rows(quantized, expand_weight)
    decoded = jax.nn.elu(pre_decoded).astype(jnp.bfloat16)
    restored = jnp.dot(decoded, decoder_weight, preferred_element_type=jnp.float32)
    frame_weight = jnp.where(
        row_length > 0, 1.0 / jnp.maximum(row_length, 1).astype(jnp.float32), 0.0
    )[:, None]
    out_grad = (2.0 * frame_weight * (restored - placed.astype(jnp.float32))).astype(jnp.bfloat16)
    grad_decoder = across_rows(decoded, out_grad)
    back_decoded = (against_rows(out_grad, decoder_weight) * elu_slope(pre_decoded)).astype(
        jnp.bfloat16
    )
    grad_expand = across_rows(back_decoded, quantized)
    decoder_part = reduce_decoder(grad_decoder, grad_expand)
    latent_grad = (
        jnp.dot(back_decoded, expand_weight, preferred_element_type=jnp.float32)
        + 2.0 * frame_weight * (latents - quantized.astype(jnp.float32))
    ).astype(jnp.bfloat16)
    grad_latent = across_rows(hidden, latent_grad)
    back_hidden = (against_rows(latent_grad, latent_weight) * elu_slope(pre_hidden)).astype(
        jnp.bfloat16
    )
    grad_encoder = across_rows(placed, back_hidden)
    return (latents, decoder_part, grad_latent, grad_encoder)


def reduce_decoder(grad_decoder, grad_expand):
    summed = (
        lax.psum_scatter(grad_decoder, ("dp", "rep"), scatter_dimension=0, tiled=True),
        lax.psum_scatter(grad_expand, ("dp", "rep"), scatter_dimension=0, tiled=True),
    )
    return summed


def reduce_encoder(grad_latent, grad_encoder):
    summed = (
        lax.psum_scatter(grad_latent, ("dp", "rep"), scatter_dimension=0, tiled=True),
        lax.psum_scatter(grad_encoder, ("dp", "rep"), scatter_dimension=0, tiled=True),
    )
    return summed


def arrival_order(place, kept_slots):
    return (
        jnp.zeros((kept_slots,), jnp.int32)
        .at[place]
        .set(jnp.arange(place.shape[0], dtype=jnp.int32), mode="drop")
    )


def per_device(
    frames,
    clip_lengths,
    block_dest,
    frame_codes,
    codebook,
    encoder_weight,
    latent_weight,
    expand_weight,
    decoder_weight,
):
    slot_count = frames.shape[0]
    block_rows = frames.shape[2]
    features = frames.shape[3]
    width_latent = latent_weight.shape[1]
    groups = lax.axis_size("dp")
    per_peer = slot_count // groups
    kept_slots = slot_count // 2
    local_frames = frames[:, 0]
    local_codes = frame_codes[:, 0]
    row_length = row_lengths(clip_lengths[0, 0])
    target = block_dest[0, 0, 0]
    place = block_dest[0, 0, 1]
    live_slot = target >= 0
    slot_index = jnp.arange(slot_count, dtype=jnp.int32)
    earlier = (
        (target[:, None] == target[None, :])
        & live_slot[None, :]
        & (slot_index[None, :] < slot_index[:, None])
    )
    peer_rank = jnp.sum(earlier.astype(jnp.int32), axis=1)
    position = jnp.where(live_slot, target * per_peer + peer_rank, slot_count)
    source = (
        jnp.full((slot_count,), slot_count - 1, jnp.int32).at[position].set(slot_index, mode="drop")
    )
    filled = jnp.zeros((slot_count,), jnp.bool_).at[position].set(True, mode="drop")
    send_place = jnp.where(filled, place[source], kept_slots)
    latents, decoder_part, grad_latent, grad_encoder = train_rows(
        local_frames.reshape(slot_count * block_rows, features),
        local_codes.reshape(-1),
        row_length.reshape(-1),
        codebook,
        encoder_weight,
        latent_weight,
        expand_weight,
        decoder_weight,
        reduce_decoder,
    )
    sent_latents = latents.reshape(slot_count, block_rows, width_latent)[source].reshape(
        groups, per_peer, block_rows, width_latent
    )
    got_latents, got_place = (
        lax.all_to_all(sent_latents, "dp", split_axis=0, concat_axis=0, tiled=True),
        lax.all_to_all(
            send_place.reshape(groups, per_peer), "dp", split_axis=0, concat_axis=0, tiled=True
        ),
    )
    order = arrival_order(got_place.reshape(-1), kept_slots)
    latent_blocks = got_latents.reshape(slot_count, block_rows, width_latent)[order].reshape(
        kept_slots, 1, block_rows, width_latent
    )
    grad_latent_out, grad_encoder_out = reduce_encoder(grad_latent, grad_encoder)
    grad_decoder_out, grad_expand_out = decoder_part
    return (latent_blocks, grad_encoder_out, grad_latent_out, grad_expand_out, grad_decoder_out)


def solution(mesh):
    in_specs = (
        P("dp", "rep", None, None),
        P("dp", "rep", None),
        P("dp", "rep", None, None),
        P("dp", "rep", None),
        P(),
        P(),
        P(),
        P(),
        P(),
    )
    out_specs = (
        P("dp", "rep", None, None),
        P(("dp", "rep"), None),
        P(("dp", "rep"), None),
        P(("dp", "rep"), None),
        P(("dp", "rep"), None),
    )
    return jax.shard_map(
        per_device, mesh=mesh, in_specs=in_specs, out_specs=out_specs, check_vma=False
    )
```

profile of v0, /device:TPU:0, one launch (start us, length us, event | category | flops | bytes accessed | tf_op | source)
XLA Modules:
  0.0 874.7 jit_solution(14378655643223248882)
XLA Ops:
  7.2 0.0 copy-start
  7.2 0.0 copy-start.2
  7.2 0.0 all-reduce.6.cloned.1.call-start
  7.2 0.8 copy.23
  8.1 0.1 reshape_squeeze.10
  8.1 0.1 reshape_squeeze.9
  8.3 0.7 and_select_fusion.1
  8.9 0.2 reduce-window.7
  9.1 0.7 broadcast_multiply_fusion
  9.8 0.7 select_reduce_fusion
  10.5 0.0 copy-done
  10.6 3.2 gather_fusion.3
  13.8 0.0 copy-done.2
  13.8 0.5 fusion.28
  14.3 8.6 multiply_convert_fusion
  22.9 6.8 fusion.7
  29.8 0.0 copy-start.4
  29.8 7.3 fusion.29
  37.1 7.1 fusion.37
  44.3 1.4 fusion.27
  45.6 0.9 fusion.34
  46.6 0.5 fusion.8
  47.0 1.7 fusion.32
  48.7 0.0 all-reduce.6.cloned.1.call-update
  48.7 0.0 reduce-scatter.4.cloned.1.call-start
  48.8 9.9 %convolution_bitcast_fusion = f32[4096,512]{0,1:T(8,128)} fusion(bf16[1024,4096]{1,0:T(8,128)(2,1)} %bitcast.77, f32[1024,512]{1,0:T(8,128)S(1)} %fusion.37, bf16[1024,128]{1,0:T(8,128)(2,1)S(1)} %fusion.8, bf16[512,128]{1,0:T(8,128)(2,1)S(1)} %copy-done.5), kind=kOutput, calls=%fused_computation.8 | convolution fusion | flops 4431806464 | bytes 19267584 | tf_op jit(solution)/shard_map/dot_general | solution.py:15
  58.6 9.4 %copy.26 = f32[4096,512]{1,0:T(8,128)} copy(f32[4096,512]{0,1:T(8,128)} %convolution_bitcast_fusion) | data formatting | bytes 16777216
  68.0 0.0 reduce-scatter.4.cloned.1.call-update
  68.1 0.7 copy-done.3
  68.7 0.2 convert_reduce_fusion
  68.9 0.8 scatter_custom_fusion
  69.7 0.8 gather_fusion.1
  70.5 0.8 scatter_custom_fusion.1
  71.3 0.7 all_to_all.10
  72.0 7.6 all-to-all-start.1
  79.6 1.5 gather_fusion
  81.1 5.8 all-to-all-done.1
  86.9 3.9 all-to-all-start
  90.8 0.5 broadcast.323
  91.3 0.7 reduce.3
  92.0 0.1 reshape.249
  92.1 0.8 scatter_custom_fusion.2
  92.9 9.1 %all-to-all-done = f32[32,2,16,128]{3,2,1,0:T(8,128)S(1)} async-done(((f32[32,2,16,128]{3,2,1,0:T(8,128)}), f32[32,2,16,128]{3,2,1,0:T(8,128)S(1)}, u32[]{:S(2)}, u32[]{:S(2)}) %all-to-all-start) | async-done | bytes 524320 | tf_op jit(solution)/shard_map/all_to_all | solution.py:155
  102.0 1.3 gather_fusion.2
  103.3 112.1 %all-reduce.6.cloned.1.call-done = (f32[512,128]{1,0:T(8,128)}, f32[512,128]{1,0:T(8,128)}, f32[512,4096]{1,0:T(8,128)}) async-done(((f32[512,128]{1,0:T(8,128)}, f32[512,128]{1,0:T(8,128)}, f32[512,4096]{1,0:T(8,128)}), (f32[512,128]{1,0:T(8,128)}, f32[512,128]{1,0:T(8,128)}, f32[512,4096]{1,0:T(8,128)})) %all-reduce.6.cloned.1.call-update) | async-done | bytes 8912912
  215.4 1.3 constant_dynamic-slice_fusion.1
  216.7 1.5 constant_dynamic-slice_fusion
  218.2 649.6 %reduce-scatter.4.cloned.1.call-done = f32[32,512]{1,0:T(8,128)} async-done(((f32[4096,512]{1,0:T(8,128)}), f32[32,512]{1,0:T(8,128)}) %reduce-scatter.4.cloned.1.call-update) | async-done | bytes 65552
  (23 shorter events, 0.1 us)
Async XLA Ops:
  7.2 3.4 copy-start
  7.2 6.6 copy-start.2
  7.2 208.2 %all-reduce.6.cloned.1.call-start = ((), (), s32[]{:S(2)}) async-start(), calls=%async_computation.4 | async-start | bytes 17825792
  29.8 7.3 copy-start.4
  37.1 8.5 copy-start.5
  48.7 819.1 %reduce-scatter.4.cloned.1.call-start = ((), (), s32[]{:S(2)}) async-start(), calls=%async_computation.3 | async-start | bytes 8454144
  68.0 0.7 copy-start.3
  68.7 799.1 %copy-start.1 = (bf16[1024,128]{1,0:T(8,128)(2,1)S(1)}, bf16[1024,128]{1,0:T(8,128)(2,1)}, u32[]{:S(2)}) copy-start(bf16[1024,128]{1,0:T(8,128)(2,1)} %param.13) | copy-start | bytes 786436
  72.0 14.9 %all-to-all-start.1 = ((s32[32,1,2]{2,1,0:T(1,128)}), s32[32,1,2]{2,1,0:T(1,128)S(1)}, u32[]{:S(2)}, u32[]{:S(2)}) async-start(s32[32,1,2]{2,1,0:T(1,128)} %bitcast.10), calls=%async_computation.1 | async-start | bytes 32768 | tf_op jit(solution)/shard_map/all_to_all | solution.py:156
  86.9 15.1 %all-to-all-start = ((f32[32,2,16,128]{3,2,1,0:T(8,128)}), f32[32,2,16,128]{3,2,1,0:T(8,128)S(1)}, u32[]{:S(2)}, u32[]{:S(2)}) async-start(f32[32,2,16,128]{3,2,1,0:T(8,128)} %bitcast.7), calls=%async_computation | async-start | bytes 1048576 | tf_op jit(solution)/shard_map/all_to_all | solution.py:155
Sparse Core Ops, SparseCore 0:
  48.8 166.5 all-reduce.5
  218.5 649.3 reduce-scatter.3
where the time goes:
time: 875 us
  waiting for transfers between devices  777 us (89%)
  matrix products  44.7 us (5%)
  local copies, waits for them, and re-layouts  24.3 us (3%)
  between operations  14.3 us (2%)
  starting transfers between devices  11.5 us (1%)
    unnamed x4, waiting for transfers between devices  762 us
    dot_general x4, matrix products, across_rows(): lax.dot_general(left, right, (((0,), (0,)), ((), ())), preferred_element_...  20.2 us
  transfers between devices with their start and end apart: 4, of which 4 were waited for; matrix products, arithmetic and copies ran while one was open for 3% of the time, Pallas kernels for 0%

commit v1 on v0

v1 whole, which is shorter than its diff:
```python
import functools

import jax
import jax.numpy as jnp
from jax import lax
from jax.experimental import pallas as pl
from jax.experimental.pallas import tpu as pltpu
from jax.sharding import PartitionSpec as P

BLK = 16
NB = 64
RB = 32
FEAT = 4096
HID = 512
LAT = 128
CODES = 1024
ROWS = NB * BLK
PEERS = 32
META = 2 * BLK + 8
DROWS = 136
TILE = 512
STEPS = FEAT // TILE
BF = jnp.bfloat16
F32 = jnp.float32
LEN, X, Y, C, Z = 0, 4, 5, 6, 7


def dot(left, right, lc, rc):
    return lax.dot_general(left, right, (((lc,), (rc,)), ((), ())), preferred_element_type=F32)


def slope_of(values):
    return jnp.exp(jnp.minimum(values, 0.0))


def iota(shape, dim):
    return lax.broadcasted_iota(jnp.int32, shape, dim)


def double_weight(scal):
    position = iota((ROWS, 1), 0)
    weight = jnp.zeros((ROWS, 1), F32)
    start = 0
    for clip in range(4):
        length = scal[LEN + clip]
        span = (length + (BLK - 1)) // BLK * BLK
        inside = (position >= start) & (position < start + length)
        share = 2.0 / jnp.full((ROWS, 1), length, jnp.int32).astype(F32)
        weight = jnp.where(inside, share, weight)
        start = start + span
    return weight


def dest_of(rank, scal):
    half, first, second, depth = rank // 64, rank // 16 % 4, rank // 4 % 4, rank % 4
    core = jnp.where(half == 0, 1 - scal[C], scal[C])
    col = (scal[X] + jnp.where(core == 0, first, second)) % 4
    row = (scal[Y] + jnp.where(core == 0, second, first)) % 4
    return ((col * 4 + row) * 2 + core) * 4 + (scal[Z] + depth) % 4


def decoder_kernel(scal, codes, codebook, expand, x, wd, og, send, keep, q_out, decoded, dec_t, w2):
    @pl.when(pl.program_id(0) == 0)
    def _():
        hot = (iota((CODES, ROWS), 0) == codes[...]).astype(BF)
        q_t = dot(codebook[...], hot, 0, 0).astype(BF)
        q = q_t.astype(F32).T.astype(BF)
        q_out[...] = q
        pre = dot(q, expand[...], 1, 1)
        decoded[...] = jnp.where(pre > 0, pre, slope_of(pre) - 1.0).astype(BF)
        source = iota((HID, 1), 0)
        source = dest_of(source // 4, scal) * 4 + source % 4
        moved = dot((iota((HID, HID), 1) == source).astype(BF), expand[...], 1, 0).astype(BF)
        pre = dot(moved, q_t, 1, 0)
        dec_t[...] = jnp.where(pre > 0, pre, slope_of(pre) - 1.0).astype(BF)
        w2[...] = double_weight(scal)

    restored = dot(decoded[...], wd[...], 1, 0)
    grad = (w2[...] * (restored - x[...].astype(F32))).astype(BF)
    og[...] = grad
    out = dot(dec_t[...], grad, 1, 0)
    send[...] = out[: HID // 2].astype(BF)
    keep[...] = out[HID // 2 :].astype(BF)


def encoder_kernel(
    scal, dest, og, wd, x, we, q_ref, expand, latent_w, bh, small, packed, back_acc, pre_acc, spread, lat, count
):
    step = pl.program_id(0)

    @pl.when(step == 0)
    def _():
        back_acc[...] = jnp.zeros_like(back_acc)
        pre_acc[...] = jnp.zeros_like(pre_acc)

    back_acc[...] += dot(og[...], wd[...], 1, 1)
    pre_acc[...] += dot(x[...], we[...], 1, 0)

    @pl.when(step == STEPS - 1)
    def _():
        q = q_ref[...]
        pre_hidden = pre_acc[...]
        hidden_slope = slope_of(pre_hidden)
        hidden = jnp.where(pre_hidden > 0, pre_hidden, hidden_slope - 1.0).astype(BF)
        latents = dot(hidden, latent_w[...], 1, 0)
        lat[...] = latents
        back = (back_acc[...] * slope_of(dot(q, expand[...], 1, 1))).astype(BF)
        grad = dot(back, expand[...], 1, 0) + double_weight(scal) * (latents - q.astype(F32))
        grad = grad.astype(BF)
        bh[...] = (dot(grad, latent_w[...], 1, 1) * hidden_slope).astype(BF)
        grad_latent = dot(grad, hidden, 0, 0).T.astype(BF)
        grad_expand = dot(q, back, 0, 0).T.astype(BF)
        both = jnp.concatenate([grad_latent, grad_expand], axis=0)
        row = iota((ROWS, 1), 0)
        source = row % 8 // 4 * HID + dest_of(row // 8, scal) * 4 + row % 4
        hot = (iota((ROWS, ROWS), 1) == source).astype(BF)
        small[...] = dot(hot, both, 1, 0).reshape(128, 8, LAT).astype(BF)

        spread[...] = jnp.zeros_like(spread)
        for peer in range(PEERS):
            count[peer] = 0

        def place(slot, _):
            target = dest[slot]

            @pl.when(target >= 0)
            def _():
                rank = count[target]
                count[target] = rank + 1
                block = lat[pl.ds(pl.multiple_of(slot * BLK, BLK), BLK), :]
                spread[target, pl.ds(pl.multiple_of(rank * BLK, BLK), BLK), :] = block
                mark = jnp.full((8, LAT), dest[NB + slot] + 1, jnp.int32).astype(F32)
                spot = iota((8, LAT), 0) == rank
                old = spread[target, 2 * BLK : META, :]
                spread[target, 2 * BLK : META, :] = jnp.where(spot, mark, old)

            return 0

        lax.fori_loop(0, NB, place, 0)
        packed[...] = spread[...].astype(BF)


def outer_kernel(scal, x, bh, small_send, small_keep, send, keep):
    out = dot(x[...], bh[...], 0, 0).astype(BF)
    mine = scal[C] == 0
    low, high = out[:128], out[128:]
    for half, ref, extra in (
        (jnp.where(mine, high, low), send, small_send),
        (jnp.where(mine, low, high), keep, small_keep),
    ):
        for depth in range(4):
            spot = (depth + 4 - scal[Z]) % 4
            for part in range(4):
                ref[spot, 32 * part : 32 * part + 32, :] = half[
                    32 * depth : 32 * depth + 32, 128 * part : 128 * part + 128
                ]
        ref[:, 128:DROWS, :] = extra[...]


def arrive_kernel(got, out):
    first = got[:, 2 * BLK, :].astype(F32)
    second = got[:, 2 * BLK + 1, :].astype(F32)
    want = (iota((PEERS, LAT), 1) + 1).astype(F32)
    hot_a = (first == want).astype(F32)[:, :RB].astype(BF)
    hot_b = (second == want).astype(F32)[:, :RB].astype(BF)
    for row in range(BLK):
        out[:, row, :] = dot(hot_a, got[:, row, :], 0, 0) + dot(hot_b, got[:, BLK + row, :], 0, 0)


def decode(scal, codes, codebook, expand, x, wd):
    whole = lambda shape: pl.BlockSpec(shape, lambda i, s: (0,) * len(shape))
    return pl.pallas_call(
        decoder_kernel,
        grid_spec=pltpu.PrefetchScalarGridSpec(
            num_scalar_prefetch=1,
            grid=(STEPS,),
            in_specs=[
                whole((1, ROWS)),
                whole((CODES, LAT)),
                whole((HID, LAT)),
                pl.BlockSpec((ROWS, TILE), lambda i, s: (0, i)),
                pl.BlockSpec((HID, TILE), lambda i, s: (0, i)),
            ],
            out_specs=[
                pl.BlockSpec((ROWS, TILE), lambda i, s: (0, i)),
                pl.BlockSpec((HID // 2, TILE), lambda i, s: (0, i)),
                pl.BlockSpec((HID // 2, TILE), lambda i, s: (0, i)),
                whole((ROWS, LAT)),
            ],
            scratch_shapes=[
                pltpu.VMEM((ROWS, HID), BF),
                pltpu.VMEM((HID, ROWS), BF),
                pltpu.VMEM((ROWS, 1), F32),
            ],
        ),
        out_shape=[
            jax.ShapeDtypeStruct((ROWS, FEAT), BF),
            jax.ShapeDtypeStruct((HID // 2, FEAT), BF),
            jax.ShapeDtypeStruct((HID // 2, FEAT), BF),
            jax.ShapeDtypeStruct((ROWS, LAT), BF),
        ],
        compiler_params=pltpu.CompilerParams(vmem_limit_bytes=40 << 20),
        cost_estimate=pl.CostEstimate(flops=9 * 10**9, bytes_accessed=24 << 20, transcendentals=0),
        name="decoder_grads",
    )(scal, codes, codebook, expand, x, wd)


def encode(scal, dest, og, wd, x, we, q, expand, latent_w):
    whole = lambda shape: pl.BlockSpec(shape, lambda i, s, d: (0,) * len(shape))
    return pl.pallas_call(
        encoder_kernel,
        grid_spec=pltpu.PrefetchScalarGridSpec(
            num_scalar_prefetch=2,
            grid=(STEPS,),
            in_specs=[
                pl.BlockSpec((ROWS, TILE), lambda i, s, d: (0, i)),
                pl.BlockSpec((HID, TILE), lambda i, s, d: (0, i)),
                pl.BlockSpec((ROWS, TILE), lambda i, s, d: (0, i)),
                pl.BlockSpec((TILE, HID), lambda i, s, d: (i, 0)),
                whole((ROWS, LAT)),
                whole((HID, LAT)),
                whole((HID, LAT)),
            ],
            out_specs=[whole((ROWS, HID)), whole((128, 8, LAT)), whole((PEERS, META, LAT))],
            scratch_shapes=[
                pltpu.VMEM((ROWS, HID), F32),
                pltpu.VMEM((ROWS, HID), F32),
                pltpu.VMEM((PEERS, META, LAT), F32),
                pltpu.VMEM((ROWS, LAT), F32),
                pltpu.SMEM((PEERS,), jnp.int32),
            ],
        ),
        out_shape=[
            jax.ShapeDtypeStruct((ROWS, HID), BF),
            jax.ShapeDtypeStruct((128, 8, LAT), BF),
            jax.ShapeDtypeStruct((PEERS, META, LAT), BF),
        ],
        compiler_params=pltpu.CompilerParams(vmem_limit_bytes=48 << 20),
        cost_estimate=pl.CostEstimate(flops=11 * 10**9, bytes_accessed=24 << 20, transcendentals=0),
        name="hidden_grads",
    )(scal, dest, og, wd, x, we, q, expand, latent_w)


def outer(scal, x, bh, small):
    def near(i, s):
        return i

    def swapped(i):
        return i % 4 * 4 + i // 4

    send_at = lambda i, s: jnp.where(s[C] == 0, swapped(i), i)
    keep_at = lambda i, s: jnp.where(s[C] == 0, i, swapped(i))
    x_at = lambda i, s: (s[X] + i // 4) % 4 * 4 + (s[Y] + i % 4) % 4
    return pl.pallas_call(
        outer_kernel,
        grid_spec=pltpu.PrefetchScalarGridSpec(
            num_scalar_prefetch=1,
            grid=(16,),
            in_specs=[
                pl.BlockSpec((ROWS, 256), lambda i, s: (0, x_at(i, s))),
                pl.BlockSpec((ROWS, HID), lambda i, s: (0, 0)),
                pl.BlockSpec((4, 8, LAT), lambda i, s: (send_at(i, s), 0, 0)),
                pl.BlockSpec((4, 8, LAT), lambda i, s: (16 + keep_at(i, s), 0, 0)),
            ],
            out_specs=[
                pl.BlockSpec((4, DROWS, LAT), lambda i, s: (send_at(i, s), 0, 0)),
                pl.BlockSpec((4, DROWS, LAT), lambda i, s: (keep_at(i, s), 0, 0)),
            ],
        ),
        out_shape=[jax.ShapeDtypeStruct((64, DROWS, LAT), BF)] * 2,
        compiler_params=pltpu.CompilerParams(vmem_limit_bytes=40 << 20),
        cost_estimate=pl.CostEstimate(flops=43 * 10**8, bytes_accessed=12 << 20, transcendentals=0),
        name="encoder_grads",
    )(scal, x, bh, small, small)


def arrive(got):
    return pl.pallas_call(
        arrive_kernel,
        out_shape=jax.ShapeDtypeStruct((RB, BLK, LAT), F32),
        name="place_latents",
    )(got)


def device(col, row, core, depth):
    return ((col * 4 + row) * 2 + core) * 4 + depth


def moves(change):
    return [
        (device(x, y, c, z), device(*change(x, y, c, z)))
        for x in range(4)
        for y in range(4)
        for c in range(2)
        for z in range(4)
    ]


def turn(phase, by):
    def change(x, y, c, z):
        if phase == 2:
            return x, y, c, (z + by) % 4
        if (phase == 0) == (c == 0):
            return (x + by) % 4, y, c, z
        return x, (y + by) % 4, c, z

    return moves(change)


BOTH = ("dp", "rep")


def reduce_scatter(send, keep):
    got = lax.ppermute(send, BOTH, moves(lambda x, y, c, z: (x, y, 1 - c, z)))
    total = keep.astype(F32) + got.astype(F32)
    for phase in range(3):
        size = total.shape[0] // 4
        arrived = [
            lax.ppermute(total[by * size : (by + 1) * size].astype(BF), BOTH, turn(phase, by))
            for by in (2, 1, 3)
        ]
        total = total[:size]
        for piece in arrived:
            total = total + piece.astype(F32)
    return total


def per_device(
    frames,
    clip_lengths,
    block_dest,
    frame_codes,
    codebook,
    encoder_weight,
    latent_weight,
    expand_weight,
    decoder_weight,
):
    dp, rep = lax.axis_index("dp"), lax.axis_index("rep")
    scal = jnp.concatenate(
        [clip_lengths.reshape(4), jnp.stack([dp // 8, dp // 2 % 4, dp % 2, rep]).astype(jnp.int32)]
    )
    x = frames.reshape(ROWS, FEAT)
    og, send, keep, q = decode(
        scal, frame_codes.reshape(1, ROWS), codebook, expand_weight, x, decoder_weight
    )
    grad_decoder = reduce_scatter(send, keep)
    bh, small, packed = encode(
        scal, block_dest.reshape(2 * NB), og, decoder_weight, x, encoder_weight, q, expand_weight, latent_weight
    )
    latents = arrive(lax.all_to_all(packed, "dp", 0, 0, tiled=True))
    send, keep = outer(scal, x, bh, small)
    total = reduce_scatter(send, keep)[0]
    grad_encoder = jnp.concatenate([total[32 * part : 32 * part + 32] for part in range(4)], axis=1)
    return latents[:, None], grad_encoder, total[128:132], total[132:136], grad_decoder


def solution(mesh):
    in_specs = (
        P("dp", "rep", None, None),
        P("dp", "rep", None),
        P("dp", "rep", None, None),
        P("dp", "rep", None),
        P(),
        P(),
        P(),
        P(),
        P(),
    )
    out_specs = (P("dp", "rep", None, None),) + (P(("dp", "rep"), None),) * 4
    return jax.shard_map(
        per_device, mesh=mesh, in_specs=in_specs, out_specs=out_specs, check_vma=False
    )
```

time: 875 us -> 133 us (0.15)
  waiting for transfers between devices: 777 us -> 22.1 us
  Pallas kernels: 0 us -> 50.1 us
  matrix products: 44.7 us -> 0 us
  starting transfers between devices: 11.5 us -> 38.5 us
  local copies, waits for them, and re-layouts: 24.3 us -> 9.82 us
  between operations: 14.3 us -> 0.79 us
    unnamed x4 -> x0, waiting for transfers between devices: 762 us -> none
    pallas_call x0 -> x4, Pallas kernels: none -> 50.1 us  [the longest x1 21.3 us: encode(): pl.pallas_call(encoder_kernel, grid_spec=pltpu.PrefetchScalarGridSpec(num...]
    dot_general x10 -> x0, matrix products: 44.7 us -> none  [the longest x4 20.2 us: across_rows(): lax.dot_general(left, right, (((0,), (0,)), ((), ())), preferred_element_...]
    ppermute x0 -> x20, starting transfers between devices: none -> 31.1 us  [the longest x18 30.6 us: reduce_scatter(): lax.ppermute(total[by * size:(by + 1) * size].astype(BF), BOTH, turn(phas...]
    ppermute x0 -> x20, waiting for transfers between devices: none -> 22.1 us  [the longest x18 22.1 us: reduce_scatter(): lax.ppermute(total[by * size:(by + 1) * size].astype(BF), BOTH, turn(phas...]
    all_to_all x2 -> x1, waiting for transfers between devices: 14.9 us -> 0.01 us  [per_device(): latents = arrive(lax.all_to_all(packed, 'dp', 0, 0, tiled=True))]
  transfers between devices with their start and end apart: 4 -> 21, of which waited for: 4 -> 7; matrix products, arithmetic and copies ran while one was open for 3% -> 7% of each run, Pallas kernels for 0% -> 26%
where the time goes in v1:
time: 133 us; the launch traced here: 132 us
  Pallas kernels  50.1 us (38%)
  starting transfers between devices  38.5 us (29%)
  waiting for transfers between devices  22.1 us (17%)
  other arithmetic  11 us (8%)
  local copies, waits for them, and re-layouts  9.82 us (7%)
    ppermute x18, starting transfers between devices, reduce_scatter(): lax.ppermute(total[by * size:(by + 1) * size].astype(BF), BOTH, turn(phas...  30.6 us
    ppermute x18, waiting for transfers between devices, reduce_scatter(): lax.ppermute(total[by * size:(by + 1) * size].astype(BF), BOTH, turn(phas...  22.1 us
    pallas_call x1, Pallas kernels, encode(): pl.pallas_call(encoder_kernel, grid_spec=pltpu.PrefetchScalarGridSpec(num...  21.3 us
    pallas_call x1, Pallas kernels, decode(): pl.pallas_call(decoder_kernel, grid_spec=pltpu.PrefetchScalarGridSpec(num...  15.6 us
    pallas_call x1, Pallas kernels, outer(): pl.pallas_call(outer_kernel, grid_spec=pltpu.PrefetchScalarGridSpec(num_s...  11 us
    all_to_all x1, starting transfers between devices, per_device(): latents = arrive(lax.all_to_all(packed, 'dp', 0, 0, tiled=True))  7.34 us
    add x2, other arithmetic, reduce_scatter(): total = keep.astype(F32) + got.astype(F32)  7.28 us
    unnamed x17, local copies, waits for them, and re-layouts  6.98 us
  transfers between devices with their start and end apart: 21, of which 7 were waited for; matrix products, arithmetic and copies ran while one was open for 7% of the time, Pallas kernels for 26%

profile of v1, /device:TPU:0, one launch (start us, length us, event | category | flops | bytes accessed | tf_op | source)
XLA Modules:
  0.0 132.2 jit_solution(16528557136423750199)
XLA Ops:
  0.7 0.8 copy.16
  1.5 0.1 reshape.30.codes
  1.5 0.7 concatenate.6.scal
  2.3 2.2 %copy-done.2 = bf16[512,4096]{1,0:T(8,128)(2,1)S(1)} copy-done((bf16[512,4096]{1,0:T(8,128)(2,1)S(1)}, bf16[512,4096]{1,0:T(8,128)(2,1)}, u32[]{:S(2)}) %copy-start.2) | copy-done | bytes 4194328
  4.5 0.9 copy-done.3
  5.4 0.9 copy-done.4
  6.3 15.6 %decoder_grads.1 = (bf16[1024,4096]{1,0:T(8,128)(2,1)}, bf16[256,4096]{1,0:T(8,128)(2,1)}, bf16[256,4096]{1,0:T(8,128)(2,1)S(1)}, bf16[1024,128]{1,0:T(8,128)(2,1)S(1)}) custom-call(s32[8]{0:T(128)S(1)} %concatenate.6.scal, s32[1,1024]{1,0:T(1,128)S(1)} %reshape.30.codes, bf16[1024,128]{1,0:T(8,128)(2,1)S(1)} %copy-done.3, bf16[512,128]{1,0:T(8,128)(2,1)S(1)} %copy-done.4, ...), custom_call_target="tpu_custom_call" | custom-call | flops 8999999488 | bytes 25165824 | tf_op jit(solution)/shard_map/decoder_grads/pallas_call | solution.py:172
  22.0 1.4 %copy-done = bf16[256,4096]{1,0:T(8,128)(2,1)} copy-done((bf16[256,4096]{1,0:T(8,128)(2,1)}, bf16[256,4096]{1,0:T(8,128)(2,1)S(1)}, u32[]{:S(2)}) %copy-start) | copy-done | bytes 2097176
  23.4 0.1 reshape.29.dest
  23.5 21.3 %hidden_grads.1 = (bf16[1024,512]{1,0:T(8,128)(2,1)S(1)}, bf16[128,8,128]{2,1,0:T(8,128)(2,1)S(1)}, bf16[32,40,128]{2,1,0:T(8,128)(2,1)}) custom-call(s32[8]{0:T(128)S(1)} %concatenate.6.scal, s32[128]{0:T(128)S(1)} %reshape.29.dest, bf16[1024,4096]{1,0:T(8,128)(2,1)} %get-tuple-element.14.og, bf16[512,4096]{1,0:T(8,128)(2,1)} %wd.3, ...), custom_call_target="tpu_custom_call" | custom-call | flops 11000000512 | bytes 25165824 | tf_op jit(solution)/shard_map/hidden_grads/pallas_call | solution.py:210
  44.8 11.0 %encoder_grads.1 = (bf16[64,136,128]{2,1,0:T(8,128)(2,1)}, bf16[64,136,128]{2,1,0:T(8,128)(2,1)S(1)}) custom-call(s32[8]{0:T(128)S(1)} %concatenate.6.scal, bf16[1024,4096]{1,0:T(8,128)(2,1)S(1)} %bitcast.25, bf16[1024,512]{1,0:T(8,128)(2,1)S(1)} %get-tuple-element.17.bh, bf16[128,8,128]{2,1,0:T(8,128)(2,1)S(1)} %get-tuple-element.18.small_send.small_keep, ...), custom_call_target="tpu_custom_call" | custom-call | flops 4300000256 | bytes 12582912 | tf_op jit(solution)/shard_map/encoder_grads/pallas_call | solution.py:254
  55.8 0.5 collective-permute-start
  56.3 7.3 %all-to-all-start = ((bf16[32,40,128]{2,1,0:T(8,128)(2,1)}), bf16[32,40,128]{2,1,0:T(8,128)(2,1)S(1)}, u32[]{:S(2)}, u32[]{:S(2)}) async-start(bf16[32,40,128]{2,1,0:T(8,128)(2,1)} %get-tuple-element.16), calls=%async_computation | async-start | bytes 655360 | tf_op jit(solution)/shard_map/all_to_all | solution.py:351
  63.6 5.1 %convert_add_fusion.1 = (f32[256,4096]{1,0:T(8,128)}, bf16[256,4096]{1,0:T(8,128)(2,1)S(1)}) fusion(bf16[256,4096]{1,0:T(8,128)(2,1)} %collective-permute-done.10, bf16[256,4096]{1,0:T(8,128)(2,1)} %copy-done), kind=kLoop, calls=%fused_computation.1 | loop fusion | flops 4194304 | bytes 10485760 | tf_op jit(solution)/shard_map/add | solution.py:315
  68.7 1.1 fusion.23
  69.8 3.3 %collective-permute-start.11 = (bf16[64,4096]{1,0:T(8,128)(2,1)}, bf16[64,4096]{1,0:T(8,128)(2,1)}, u32[]{:S(2)}, u32[]{:S(2)}) collective-permute-start(bf16[64,4096]{1,0:T(8,128)(2,1)} %get-tuple-element.48), channel_id=1, source_target_pairs={{0,64},{1,65},{2,66},{3,67},{4,20},{5,21},{6,22},{7,23},{8,72},{9,... | collective-permute-start | bytes 1572872 | tf_op jit(solution)/shard_map/ppermute | solution.py:319
  73.1 1.2 collective-permute-start.13
  74.3 0.9 collective-permute-start.12
  75.2 0.7 copy-done.6
  75.9 2.2 %place_latents.1 = f32[32,16,128]{2,1,0:T(8,128)} custom-call(bf16[32,40,128]{2,1,0:T(8,128)(2,1)} %copy-done.6), custom_call_target="tpu_custom_call" | custom-call | tf_op jit(solution)/shard_map/place_latents/pallas_call | solution.py:278
  78.1 2.2 %convert_add_fusion = (f32[64,136,128]{2,1,0:T(8,128)S(1)}, bf16[64,136,128]{2,1,0:T(8,128)(2,1)S(1)}) fusion(bf16[64,136,128]{2,1,0:T(8,128)(2,1)} %collective-permute-done, bf16[64,136,128]{2,1,0:T(8,128)(2,1)S(1)} %get-tuple-element.19), kind=kLoop, calls=%fused_computation | loop fusion | flops 4456448 | bytes 11141120 | tf_op jit(solution)/shard_map/add | solution.py:315
  80.3 0.7 collective-permute-done.11
  80.9 5.9 %collective-permute-done.13 = bf16[64,4096]{1,0:T(8,128)(2,1)} collective-permute-done((bf16[64,4096]{1,0:T(8,128)(2,1)}, bf16[64,4096]{1,0:T(8,128)(2,1)}, u32[]{:S(2)}, u32[]{:S(2)}) %collective-permute-start.13) | collective-permute-done | bytes 524320 | tf_op jit(solution)/shard_map/ppermute | solution.py:319
  86.9 1.9 %fusion.16 = (bf16[64,4096]{1,0:T(8,128)(2,1)S(1)}, f32[64,4096]{1,0:T(8,128)S(1)}) fusion(bf16[64,4096]{1,0:T(8,128)(2,1)} %collective-permute-done.13, bf16[64,4096]{1,0:T(8,128)(2,1)} %collective-permute-done.12, bf16[64,4096]{1,0:T(8,128)(2,1)} %collective-permute-done.11, f32[256,4096]{1,0:T(8,128)} %get-tuple-element.43), kind=kLoop, calls=%fused_computation.30 | loop fusion | flops 1835008 | bytes 4194304 | tf_op jit(solution)/shard_map/convert.5
  88.9 3.1 %collective-permute-start.14 = (bf16[16,4096]{1,0:T(8,128)(2,1)S(1)}, bf16[16,4096]{1,0:T(8,128)(2,1)S(1)}, u32[]{:S(2)}, u32[]{:S(2)}) collective-permute-start(bf16[16,4096]{1,0:T(8,128)(2,1)S(1)} %get-tuple-element.54), channel_id=1, source_target_pairs={{0,16},{1,17},{2,18},{3,19},{4,68},{5,69},{6,70},{7,71},{8,24},{9,... | collective-permute-start | bytes 393224 | tf_op jit(solution)/shard_map/ppermute | solution.py:319
  91.9 1.2 collective-permute-start.16
  93.1 0.9 collective-permute-start.15
  94.0 0.1 fusion.22
  94.1 2.9 %collective-permute-start.1 = (bf16[16,136,128]{2,1,0:T(8,128)(2,1)S(1)}, bf16[16,136,128]{2,1,0:T(8,128)(2,1)S(1)}, u32[]{:S(2)}, u32[]{:S(2)}) collective-permute-start(bf16[16,136,128]{2,1,0:T(8,128)(2,1)S(1)} %get-tuple-element.45), channel_id=1, source_target_pairs={{0,64},{1,65},{2,66},{3,67},{4,20},{5,21},{6,22},{7,23},{8,72},{9,... | collective-permute-start | bytes 1671176 | tf_op jit(solution)/shard_map/ppermute | solution.py:319
  97.0 1.2 collective-permute-start.3
  98.2 0.8 collective-permute-start.2
  99.1 6.5 %collective-permute-done.15 = bf16[16,4096]{1,0:T(8,128)(2,1)S(1)} collective-permute-done((bf16[16,4096]{1,0:T(8,128)(2,1)S(1)}, bf16[16,4096]{1,0:T(8,128)(2,1)S(1)}, u32[]{:S(2)}, u32[]{:S(2)}) %collective-permute-start.15) | collective-permute-done | bytes 131104 | tf_op jit(solution)/shard_map/ppermute | solution.py:319
  105.6 5.5 %collective-permute-done.3 = bf16[16,136,128]{2,1,0:T(8,128)(2,1)S(1)} collective-permute-done((bf16[16,136,128]{2,1,0:T(8,128)(2,1)S(1)}, bf16[16,136,128]{2,1,0:T(8,128)(2,1)S(1)}, u32[]{:S(2)}, u32[]{:S(2)}) %collective-permute-start.3) | collective-permute-done | bytes 557088 | tf_op jit(solution)/shard_map/ppermute | solution.py:319
  111.2 0.3 fusion.20
  111.5 0.7 collective-permute-start.4
  112.2 2.6 %collective-permute-start.6 = (bf16[4,136,128]{2,1,0:T(8,128)(2,1)S(1)}, bf16[4,136,128]{2,1,0:T(8,128)(2,1)S(1)}, u32[]{:S(2)}, u32[]{:S(2)}) collective-permute-start(bf16[4,136,128]{2,1,0:T(8,128)(2,1)S(1)} %get-tuple-element.52), channel_id=1, source_target_pairs={{0,24},{1,25},{2,26},{3,27},{4,100},{5,101},{6,102},{7,103},{8,0},... | collective-permute-start | bytes 417800 | tf_op jit(solution)/shard_map/ppermute | solution.py:319
  114.9 3.9 %collective-permute-start.17 = (bf16[4,4096]{1,0:T(4,128)(2,1)S(1)}, bf16[4,4096]{1,0:T(4,128)(2,1)S(1)}, u32[]{:S(2)}, u32[]{:S(2)}) collective-permute-start(bf16[4,4096]{1,0:T(4,128)(2,1)S(1)} %get-tuple-element.60), channel_id=1, source_target_pairs={{0,2},{1,3},{2,0},{3,1},{4,6},{5,7},{6,4},{7,5},{8,10},{9,11},{10,... | collective-permute-start | bytes 98312 | tf_op jit(solution)/shard_map/ppermute | solution.py:319
  118.8 0.7 collective-permute-start.19
  119.5 1.3 %collective-permute-start.18 = (bf16[4,4096]{1,0:T(4,128)(2,1)S(1)}, bf16[4,4096]{1,0:T(4,128)(2,1)S(1)}, u32[]{:S(2)}, u32[]{:S(2)}) collective-permute-start(bf16[4,4096]{1,0:T(4,128)(2,1)S(1)} %get-tuple-element.62), channel_id=1, source_target_pairs={{0,1},{1,2},{2,3},{3,0},{4,5},{5,6},{6,7},{7,4},{8,9},{9,10},{10,1... | collective-permute-start | bytes 98312 | tf_op jit(solution)/shard_map/ppermute | solution.py:319
  120.8 0.3 collective-permute-done.5
  121.2 3.9 %collective-permute-start.7 = (bf16[1,136,128]{2,1,0:T(8,128)(2,1)S(1)}, bf16[1,136,128]{2,1,0:T(8,128)(2,1)S(1)}, u32[]{:S(2)}, u32[]{:S(2)}) collective-permute-start(bf16[1,136,128]{2,1,0:T(8,128)(2,1)S(1)} %get-tuple-element.57), channel_id=1, source_target_pairs={{0,2},{1,3},{2,0},{3,1},{4,6},{5,7},{6,4},{7,5},{8,10},{9,11},{10,... | collective-permute-start | bytes 104456 | tf_op jit(solution)/shard_map/ppermute | solution.py:319
  125.1 0.7 collective-permute-start.9
  125.8 1.3 %collective-permute-start.8 = (bf16[1,136,128]{2,1,0:T(8,128)(2,1)S(1)}, bf16[1,136,128]{2,1,0:T(8,128)(2,1)S(1)}, u32[]{:S(2)}, u32[]{:S(2)}) collective-permute-start(bf16[1,136,128]{2,1,0:T(8,128)(2,1)S(1)} %get-tuple-element.59), channel_id=1, source_target_pairs={{0,1},{1,2},{2,3},{3,0},{4,5},{5,6},{6,7},{7,4},{8,9},{9,10},{10,1... | collective-permute-start | bytes 104456 | tf_op jit(solution)/shard_map/ppermute | solution.py:319
  127.1 0.7 fusion.11
  127.8 1.2 collective-permute-done.9
  129.0 1.9 %collective-permute-done.8 = bf16[1,136,128]{2,1,0:T(8,128)(2,1)S(1)} collective-permute-done((bf16[1,136,128]{2,1,0:T(8,128)(2,1)S(1)}, bf16[1,136,128]{2,1,0:T(8,128)(2,1)S(1)}, u32[]{:S(2)}, u32[]{:S(2)}) %collective-permute-start.8) | collective-permute-done | bytes 34848 | tf_op jit(solution)/shard_map/ppermute | solution.py:319
  131.0 0.6 slice_bitcast_fusion.4
  131.6 0.6 pad_maximum_fusion
  (35 shorter events, 0.3 us)
Async XLA Ops:
  2.3 2.2 %copy-start.2 = (bf16[512,4096]{1,0:T(8,128)(2,1)S(1)}, bf16[512,4096]{1,0:T(8,128)(2,1)}, u32[]{:S(2)}) copy-start(bf16[512,4096]{1,0:T(8,128)(2,1)} %wd.3) | copy-start | bytes 12582916
  4.5 0.9 copy-start.3
  5.4 0.9 copy-start.4
  6.3 17.1 %copy-start.7 = (s32[1,1,2,64]{3,2,1,0:T(2,128)S(1)}, s32[1,1,2,64]{3,2,1,0:T(2,128)}, u32[]{:S(2)}) copy-start(s32[1,1,2,64]{3,2,1,0:T(2,128)} %param.11) | copy-start | bytes 1540
  6.3 17.1 %copy-start.5 = (bf16[512,128]{1,0:T(8,128)(2,1)S(1)}, bf16[512,128]{1,0:T(8,128)(2,1)}, u32[]{:S(2)}) copy-start(bf16[512,128]{1,0:T(8,128)(2,1)} %latent_w.1) | copy-start | bytes 393220
  22.0 1.4 %copy-start = (bf16[256,4096]{1,0:T(8,128)(2,1)}, bf16[256,4096]{1,0:T(8,128)(2,1)S(1)}, u32[]{:S(2)}) copy-start(bf16[256,4096]{1,0:T(8,128)(2,1)S(1)} %get-tuple-element.21) | copy-start | bytes 6291460
  23.4 40.3 %collective-permute-start.10 = (bf16[256,4096]{1,0:T(8,128)(2,1)}, bf16[256,4096]{1,0:T(8,128)(2,1)}, u32[]{:S(2)}, u32[]{:S(2)}) collective-permute-start(bf16[256,4096]{1,0:T(8,128)(2,1)} %get-tuple-element.22), channel_id=1, source_target_pairs={{0,4},{1,5},{2,6},{3,7},{4,0},{5,1},{6,2},{7,3},{8,12},{9,13},{10,... | collective-permute-start | bytes 6291464 | tf_op jit(solution)/shard_map/ppermute | solution.py:314
  23.5 21.3 %copy-start.1 = (bf16[64,1,16,4096]{3,2,1,0:T(8,128)(2,1)S(1)}, bf16[64,1,16,4096]{3,2,1,0:T(8,128)(2,1)}, u32[]{:S(2)}) copy-start(bf16[64,1,16,4096]{3,2,1,0:T(8,128)(2,1)} %param.9) | copy-start | bytes 25165828
  55.8 22.3 %collective-permute-start = (bf16[64,136,128]{2,1,0:T(8,128)(2,1)}, bf16[64,136,128]{2,1,0:T(8,128)(2,1)}, u32[]{:S(2)}, u32[]{:S(2)}) collective-permute-start(bf16[64,136,128]{2,1,0:T(8,128)(2,1)} %get-tuple-element.20), channel_id=1, source_target_pairs={{0,4},{1,5},{2,6},{3,7},{4,0},{5,1},{6,2},{7,3},{8,12},{9,13},{10,... | collective-permute-start | bytes 6684680 | tf_op jit(solution)/shard_map/ppermute | solution.py:314
  56.3 18.9 %all-to-all-start = ((bf16[32,40,128]{2,1,0:T(8,128)(2,1)}), bf16[32,40,128]{2,1,0:T(8,128)(2,1)S(1)}, u32[]{:S(2)}, u32[]{:S(2)}) async-start(bf16[32,40,128]{2,1,0:T(8,128)(2,1)} %get-tuple-element.16), calls=%async_computation | async-start | bytes 655360 | tf_op jit(solution)/shard_map/all_to_all | solution.py:351
  69.8 11.1 %collective-permute-start.11 = (bf16[64,4096]{1,0:T(8,128)(2,1)}, bf16[64,4096]{1,0:T(8,128)(2,1)}, u32[]{:S(2)}, u32[]{:S(2)}) collective-permute-start(bf16[64,4096]{1,0:T(8,128)(2,1)} %get-tuple-element.48), channel_id=1, source_target_pairs={{0,64},{1,65},{2,66},{3,67},{4,20},{5,21},{6,22},{7,23},{8,72},{9,... | collective-permute-start | bytes 1572872 | tf_op jit(solution)/shard_map/ppermute | solution.py:319
  73.1 13.7 %collective-permute-start.13 = (bf16[64,4096]{1,0:T(8,128)(2,1)}, bf16[64,4096]{1,0:T(8,128)(2,1)}, u32[]{:S(2)}, u32[]{:S(2)}) collective-permute-start(bf16[64,4096]{1,0:T(8,128)(2,1)} %get-tuple-element.49), channel_id=1, source_target_pairs={{0,96},{1,97},{2,98},{3,99},{4,28},{5,29},{6,30},{7,31},{8,104},{9... | collective-permute-start | bytes 1572872 | tf_op jit(solution)/shard_map/ppermute | solution.py:319
  74.3 12.6 %collective-permute-start.12 = (bf16[64,4096]{1,0:T(8,128)(2,1)S(1)}, bf16[64,4096]{1,0:T(8,128)(2,1)}, u32[]{:S(2)}, u32[]{:S(2)}) collective-permute-start(bf16[64,4096]{1,0:T(8,128)(2,1)S(1)} %get-tuple-element.50), channel_id=1, source_target_pairs={{0,32},{1,33},{2,34},{3,35},{4,12},{5,13},{6,14},{7,15},{8,40},{9,... | collective-permute-start | bytes 1572872 | tf_op jit(solution)/shard_map/ppermute | solution.py:319
  75.2 0.7 copy-start.6
  88.9 9.4 %collective-permute-start.14 = (bf16[16,4096]{1,0:T(8,128)(2,1)S(1)}, bf16[16,4096]{1,0:T(8,128)(2,1)S(1)}, u32[]{:S(2)}, u32[]{:S(2)}) collective-permute-start(bf16[16,4096]{1,0:T(8,128)(2,1)S(1)} %get-tuple-element.54), channel_id=1, source_target_pairs={{0,16},{1,17},{2,18},{3,19},{4,68},{5,69},{6,70},{7,71},{8,24},{9,... | collective-permute-start | bytes 393224 | tf_op jit(solution)/shard_map/ppermute | solution.py:319
  91.9 7.1 %collective-permute-start.16 = (bf16[16,4096]{1,0:T(8,128)(2,1)S(1)}, bf16[16,4096]{1,0:T(8,128)(2,1)S(1)}, u32[]{:S(2)}, u32[]{:S(2)}) collective-permute-start(bf16[16,4096]{1,0:T(8,128)(2,1)S(1)} %get-tuple-element.55), channel_id=1, source_target_pairs={{0,24},{1,25},{2,26},{3,27},{4,100},{5,101},{6,102},{7,103},{8,0},... | collective-permute-start | bytes 393224 | tf_op jit(solution)/shard_map/ppermute | solution.py:319
  93.1 12.5 %collective-permute-start.15 = (bf16[16,4096]{1,0:T(8,128)(2,1)S(1)}, bf16[16,4096]{1,0:T(8,128)(2,1)S(1)}, u32[]{:S(2)}, u32[]{:S(2)}) collective-permute-start(bf16[16,4096]{1,0:T(8,128)(2,1)S(1)} %get-tuple-element.56), channel_id=1, source_target_pairs={{0,8},{1,9},{2,10},{3,11},{4,36},{5,37},{6,38},{7,39},{8,16},{9,17... | collective-permute-start | bytes 393224 | tf_op jit(solution)/shard_map/ppermute | solution.py:319
  94.1 11.5 %collective-permute-start.1 = (bf16[16,136,128]{2,1,0:T(8,128)(2,1)S(1)}, bf16[16,136,128]{2,1,0:T(8,128)(2,1)S(1)}, u32[]{:S(2)}, u32[]{:S(2)}) collective-permute-start(bf16[16,136,128]{2,1,0:T(8,128)(2,1)S(1)} %get-tuple-element.45), channel_id=1, source_target_pairs={{0,64},{1,65},{2,66},{3,67},{4,20},{5,21},{6,22},{7,23},{8,72},{9,... | collective-permute-start | bytes 1671176 | tf_op jit(solution)/shard_map/ppermute | solution.py:319
  97.0 14.1 %collective-permute-start.3 = (bf16[16,136,128]{2,1,0:T(8,128)(2,1)S(1)}, bf16[16,136,128]{2,1,0:T(8,128)(2,1)S(1)}, u32[]{:S(2)}, u32[]{:S(2)}) collective-permute-start(bf16[16,136,128]{2,1,0:T(8,128)(2,1)S(1)} %get-tuple-element.46), channel_id=1, source_target_pairs={{0,96},{1,97},{2,98},{3,99},{4,28},{5,29},{6,30},{7,31},{8,104},{9... | collective-permute-start | bytes 1671176 | tf_op jit(solution)/shard_map/ppermute | solution.py:319
  98.2 12.9 %collective-permute-start.2 = (bf16[16,136,128]{2,1,0:T(8,128)(2,1)S(1)}, bf16[16,136,128]{2,1,0:T(8,128)(2,1)S(1)}, u32[]{:S(2)}, u32[]{:S(2)}) collective-permute-start(bf16[16,136,128]{2,1,0:T(8,128)(2,1)S(1)} %get-tuple-element.47), channel_id=1, source_target_pairs={{0,32},{1,33},{2,34},{3,35},{4,12},{5,13},{6,14},{7,15},{8,40},{9,... | collective-permute-start | bytes 1671176 | tf_op jit(solution)/shard_map/ppermute | solution.py:319
  111.5 8.0 %collective-permute-start.4 = (bf16[4,136,128]{2,1,0:T(8,128)(2,1)S(1)}, bf16[4,136,128]{2,1,0:T(8,128)(2,1)S(1)}, u32[]{:S(2)}, u32[]{:S(2)}) collective-permute-start(bf16[4,136,128]{2,1,0:T(8,128)(2,1)S(1)} %get-tuple-element.51), channel_id=1, source_target_pairs={{0,16},{1,17},{2,18},{3,19},{4,68},{5,69},{6,70},{7,71},{8,24},{9,... | collective-permute-start | bytes 417800 | tf_op jit(solution)/shard_map/ppermute | solution.py:319
  112.2 8.6 %collective-permute-start.6 = (bf16[4,136,128]{2,1,0:T(8,128)(2,1)S(1)}, bf16[4,136,128]{2,1,0:T(8,128)(2,1)S(1)}, u32[]{:S(2)}, u32[]{:S(2)}) collective-permute-start(bf16[4,136,128]{2,1,0:T(8,128)(2,1)S(1)} %get-tuple-element.52), channel_id=1, source_target_pairs={{0,24},{1,25},{2,26},{3,27},{4,100},{5,101},{6,102},{7,103},{8,0},... | collective-permute-start | bytes 417800 | tf_op jit(solution)/shard_map/ppermute | solution.py:319
  114.8 6.3 %collective-permute-start.5 = (bf16[4,136,128]{2,1,0:T(8,128)(2,1)S(1)}, bf16[4,136,128]{2,1,0:T(8,128)(2,1)S(1)}, u32[]{:S(2)}, u32[]{:S(2)}) collective-permute-start(bf16[4,136,128]{2,1,0:T(8,128)(2,1)S(1)} %get-tuple-element.53), channel_id=1, source_target_pairs={{0,8},{1,9},{2,10},{3,11},{4,36},{5,37},{6,38},{7,39},{8,16},{9,17... | collective-permute-start | bytes 417800 | tf_op jit(solution)/shard_map/ppermute | solution.py:319
  114.9 10.9 %collective-permute-start.17 = (bf16[4,4096]{1,0:T(4,128)(2,1)S(1)}, bf16[4,4096]{1,0:T(4,128)(2,1)S(1)}, u32[]{:S(2)}, u32[]{:S(2)}) collective-permute-start(bf16[4,4096]{1,0:T(4,128)(2,1)S(1)} %get-tuple-element.60), channel_id=1, source_target_pairs={{0,2},{1,3},{2,0},{3,1},{4,6},{5,7},{6,4},{7,5},{8,10},{9,11},{10,... | collective-permute-start | bytes 98312 | tf_op jit(solution)/shard_map/ppermute | solution.py:319
  118.8 8.3 %collective-permute-start.19 = (bf16[4,4096]{1,0:T(4,128)(2,1)S(1)}, bf16[4,4096]{1,0:T(4,128)(2,1)S(1)}, u32[]{:S(2)}, u32[]{:S(2)}) collective-permute-start(bf16[4,4096]{1,0:T(4,128)(2,1)S(1)} %get-tuple-element.61), channel_id=1, source_target_pairs={{0,3},{1,0},{2,1},{3,2},{4,7},{5,4},{6,5},{7,6},{8,11},{9,8},{10,9... | collective-permute-start | bytes 98312 | tf_op jit(solution)/shard_map/ppermute | solution.py:319
  119.5 7.6 %collective-permute-start.18 = (bf16[4,4096]{1,0:T(4,128)(2,1)S(1)}, bf16[4,4096]{1,0:T(4,128)(2,1)S(1)}, u32[]{:S(2)}, u32[]{:S(2)}) collective-permute-start(bf16[4,4096]{1,0:T(4,128)(2,1)S(1)} %get-tuple-element.62), channel_id=1, source_target_pairs={{0,1},{1,2},{2,3},{3,0},{4,5},{5,6},{6,7},{7,4},{8,9},{9,10},{10,1... | collective-permute-start | bytes 98312 | tf_op jit(solution)/shard_map/ppermute | solution.py:319
  121.2 6.6 %collective-permute-start.7 = (bf16[1,136,128]{2,1,0:T(8,128)(2,1)S(1)}, bf16[1,136,128]{2,1,0:T(8,128)(2,1)S(1)}, u32[]{:S(2)}, u32[]{:S(2)}) collective-permute-start(bf16[1,136,128]{2,1,0:T(8,128)(2,1)S(1)} %get-tuple-element.57), channel_id=1, source_target_pairs={{0,2},{1,3},{2,0},{3,1},{4,6},{5,7},{6,4},{7,5},{8,10},{9,11},{10,... | collective-permute-start | bytes 104456 | tf_op jit(solution)/shard_map/ppermute | solution.py:319
  125.1 3.9 %collective-permute-start.9 = (bf16[1,136,128]{2,1,0:T(8,128)(2,1)S(1)}, bf16[1,136,128]{2,1,0:T(8,128)(2,1)S(1)}, u32[]{:S(2)}, u32[]{:S(2)}) collective-permute-start(bf16[1,136,128]{2,1,0:T(8,128)(2,1)S(1)} %get-tuple-element.58), channel_id=1, source_target_pairs={{0,3},{1,0},{2,1},{3,2},{4,7},{5,4},{6,5},{7,6},{8,11},{9,8},{10,9... | collective-permute-start | bytes 104456 | tf_op jit(solution)/shard_map/ppermute | solution.py:319
  125.8 5.1 %collective-permute-start.8 = (bf16[1,136,128]{2,1,0:T(8,128)(2,1)S(1)}, bf16[1,136,128]{2,1,0:T(8,128)(2,1)S(1)}, u32[]{:S(2)}, u32[]{:S(2)}) collective-permute-start(bf16[1,136,128]{2,1,0:T(8,128)(2,1)S(1)} %get-tuple-element.59), channel_id=1, source_target_pairs={{0,1},{1,2},{2,3},{3,0},{4,5},{5,6},{6,7},{7,4},{8,9},{9,10},{10,1... | collective-permute-start | bytes 104456 | tf_op jit(solution)/shard_map/ppermute | solution.py:319

commit v2 on v1

v2 whole, which is shorter than its diff:
```python
import functools

import jax
import jax.numpy as jnp
from jax import lax
from jax.experimental import pallas as pl
from jax.experimental.pallas import tpu as pltpu
from jax.sharding import PartitionSpec as P

BLK = 16
NB = 64
RB = 32
FEAT = 4096
HID = 512
LAT = 128
CODES = 1024
ROWS = NB * BLK
PEERS = 32
META = 2 * BLK + 8
DROWS = 136
JROWS = DROWS + 128
TILE = 512
STEPS = FEAT // TILE
BF = jnp.bfloat16
F32 = jnp.float32
X, Y, C, Z = range(4)


def dot(left, right, lc, rc):
    return lax.dot_general(left, right, (((lc,), (rc,)), ((), ())), preferred_element_type=F32)


def slope_of(values):
    return jnp.exp(jnp.minimum(values, 0.0))


def iota(shape, dim):
    return lax.broadcasted_iota(jnp.int32, shape, dim)


def place_of_device():
    dp = lax.axis_index("dp")
    return dp >> 3, dp >> 1 & 3, dp & 1, lax.axis_index("rep")


def double_weight(lengths):
    position = iota((ROWS, 1), 0)
    weight = jnp.zeros((ROWS, 1), F32)
    start = 0
    for clip in range(4):
        length = lengths[clip]
        span = (length + (BLK - 1)) // BLK * BLK
        inside = (position >= start) & (position < start + length)
        share = 2.0 / jnp.full((ROWS, 1), length, jnp.int32).astype(F32)
        weight = jnp.where(inside, share, weight)
        start = start + span
    return weight


def dest_of(rank, scal):
    first, second = rank >> 4, rank >> 2
    core = (1 - (rank >> 6)) ^ scal[C]
    near = 1 + 2 * core
    far = 3 - 2 * core
    col = scal[X] ^ ((first >> 1 & 1) * near) ^ ((second >> 1 & 1) * far)
    row = scal[Y] ^ ((first & 1) * near) ^ ((second & 1) * far)
    return ((col * 4 + row) * 2 + core) * 4 + ((scal[Z] + rank) & 3)


def main_kernel(
    lengths, codes, codebook, expand, latent_w, x, wd, we,
    send, keep, bh, lat, small,
    q_s, decoded, dec_t, w2, back_acc, pre_acc, order,
):
    step = pl.program_id(0)
    scal = place_of_device()

    @pl.when(step == 0)
    def _():
        by_slot = codes[:, 0, :]
        spread = (iota((BLK, ROWS), 1) & (BLK - 1) == iota((BLK, ROWS), 0)).astype(BF)
        high = dot((by_slot >> 5).astype(F32).astype(BF), spread, 1, 0)
        low = dot((by_slot & 31).astype(F32).astype(BF), spread, 1, 0)
        mine = iota((NB, ROWS), 1) >> 4 == iota((NB, ROWS), 0)
        row = jnp.sum(jnp.where(mine, high * 32.0 + low, 0.0), axis=0, keepdims=True).astype(jnp.int32)
        hot = (iota((CODES, ROWS), 0) == row).astype(BF)
        q_t = dot(codebook[...], hot, 0, 0).astype(BF)
        q = q_t.astype(F32).T.astype(BF)
        q_s[...] = q
        pre = dot(q, expand[...], 1, 1)
        decoded[...] = jnp.where(pre > 0, pre, slope_of(pre) - 1.0).astype(BF)
        source = iota((HID, 1), 0)
        source = dest_of(source >> 2, scal) * 4 + (source & 3)
        order[...] = (iota((HID, HID), 1) == source).astype(BF)
        moved = dot(order[...], expand[...], 1, 0).astype(BF)
        pre = dot(moved, q_t, 1, 0)
        dec_t[...] = jnp.where(pre > 0, pre, slope_of(pre) - 1.0).astype(BF)
        w2[...] = double_weight(lengths)
        back_acc[...] = jnp.zeros_like(back_acc)
        pre_acc[...] = jnp.zeros_like(pre_acc)

    restored = dot(decoded[...], wd[...], 1, 0)
    pre_acc[...] += dot(x[...], we[...], 1, 0)
    grad = (w2[...] * (restored - x[...].astype(F32))).astype(BF)
    out = dot(dec_t[...], grad, 1, 0)
    send[...] = out[: HID // 2].astype(BF)
    keep[...] = out[HID // 2 :].astype(BF)
    back_acc[...] += dot(grad, wd[...], 1, 1)

    @pl.when(step == STEPS - 1)
    def _():
        q = q_s[...]
        pre_hidden = pre_acc[...]
        hidden_slope = slope_of(pre_hidden)
        hidden = jnp.where(pre_hidden > 0, pre_hidden, hidden_slope - 1.0).astype(BF)
        latents = dot(hidden, latent_w[...], 1, 0)
        lat[...] = latents
        back = (back_acc[...] * slope_of(dot(q, expand[...], 1, 1))).astype(BF)
        grad = dot(back, expand[...], 1, 0) + w2[...] * (latents - q.astype(F32))
        grad = grad.astype(BF)
        bh[...] = (dot(grad, latent_w[...], 1, 1) * hidden_slope).astype(BF)
        grad_latent = dot(grad, hidden, 0, 0).T.astype(BF)
        grad_expand = dot(q, back, 0, 0).T.astype(BF)
        grad_latent = dot(order[...], grad_latent, 1, 0)
        grad_expand = dot(order[...], grad_expand, 1, 0)
        upper = iota((8, LAT), 0) < 4
        for pair in range(64):
            left, right = grad_latent[8 * pair : 8 * pair + 8], grad_expand[8 * pair : 8 * pair + 8]
            small[2 * pair] = jnp.where(upper, left, pltpu.roll(right, 4, 0)).astype(BF)
            small[2 * pair + 1] = jnp.where(upper, pltpu.roll(left, 4, 0), right).astype(BF)


def pack_kernel(dest, lat, _, packed, spread, count):
    spread[...] = jnp.zeros_like(spread)
    for peer in range(PEERS):
        count[peer] = 0

    def place(slot, _):
        target = dest[slot]

        @pl.when(target >= 0)
        def _():
            rank = count[target]
            count[target] = rank + 1
            block = lat[pl.ds(pl.multiple_of(slot * BLK, BLK), BLK), :]
            spread[target, pl.ds(pl.multiple_of(rank * BLK, BLK), BLK), :] = block
            mark = jnp.full((8, LAT), dest[NB + slot] + 1, jnp.int32).astype(F32)
            spot = iota((8, LAT), 0) == rank
            old = spread[target, 2 * BLK : META, :]
            spread[target, 2 * BLK : META, :] = jnp.where(spot, mark, old)

        return 0

    lax.fori_loop(0, NB, place, 0)
    packed[...] = spread[...].astype(BF)


def outer_kernel(x, bh, small, send, keep):
    scal = place_of_device()
    step = pl.program_id(0)
    for half, out in ((0, send), (1, keep)):
        core = scal[C] if half else 1 - scal[C]
        near = 1 + 2 * core
        wide = [x[:, pl.ds(pl.multiple_of(256 * row + 128 * core, 128), 128)] for row in range(4)]
        grad = dot(jnp.concatenate(wide, axis=1), bh[...], 0, 0).astype(BF)

        def bits(relative):
            middle = relative == 2
            first = (middle | (relative == near)).astype(jnp.int32)
            return first, (middle | (relative == 4 - near)).astype(jnp.int32)

        col_first, col_second = bits(step ^ scal[X])
        for row in range(4):
            row_first, row_second = bits(row ^ scal[Y])
            base = ((col_first * 2 + row_first) * 4 + col_second * 2 + row_second) * 4
            for depth in range(4):
                spot = base + ((depth + 4 - scal[Z]) & 3)
                top = 128 * row + 32 * depth
                for part in range(4):
                    out[spot, 32 * part : 32 * part + 32, :] = grad[top : top + 32, 128 * part : 128 * part + 128]

    @pl.when(step == 3)
    def _():
        send[:, 128:DROWS, :] = small[:64]
        keep[:, 128:DROWS, :] = small[64:]


def join_kernel(own_e, e3, e2, e1, own_d, d3, d2, d1, own, s1, s2, s3, acc):
    total = own_e[...]
    for piece in (e3, e2, e1):
        total = total + piece[...].astype(F32)
    acc[:, :DROWS, :] = total
    upper = iota((8, LAT), 0) < 4
    for pair in range(8):
        rows = slice(8 * pair, 8 * pair + 8)
        total = own_d[rows, :]
        for piece in (d3, d2, d1):
            total = total + piece[rows, :].astype(F32)
        for cols in range(16):
            left = total[:, 256 * cols : 256 * cols + 128]
            right = total[:, 256 * cols + 128 : 256 * cols + 256]
            spot = slice(DROWS + 8 * cols, DROWS + 8 * cols + 8)
            acc[2 * pair, spot, :] = jnp.where(upper, left, pltpu.roll(right, 4, 0))
            acc[2 * pair + 1, spot, :] = jnp.where(upper, pltpu.roll(left, 4, 0), right)
    own[...] = acc[0:4]
    s1[...] = acc[4:8].astype(BF)
    s2[...] = acc[8:12].astype(BF)
    s3[...] = acc[12:16].astype(BF)


def last_kernel(own, a3, a2, a1, enc, lat, exp, dec):
    total = own[0]
    for piece in (a3, a2, a1):
        total = total + piece[0].astype(F32)
    for part in range(4):
        enc[:, 128 * part : 128 * part + 128] = total[32 * part : 32 * part + 32]
    tail = total[128:DROWS]
    lat[...] = tail[:4]
    exp[...] = tail[4:]
    for cols in range(32):
        dec[:, 128 * cols : 128 * cols + 128] = total[DROWS + 4 * cols : DROWS + 4 * cols + 4]


def arrive_kernel(got, out):
    first = got[:, 2 * BLK, :].astype(F32)
    second = got[:, 2 * BLK + 1, :].astype(F32)
    want = (iota((PEERS, LAT), 1) + 1).astype(F32)
    hot_a = (first == want).astype(F32)[:, :RB].astype(BF)
    hot_b = (second == want).astype(F32)[:, :RB].astype(BF)
    for row in range(BLK):
        out[:, row, :] = dot(hot_a, got[:, row, :], 0, 0) + dot(hot_b, got[:, BLK + row, :], 0, 0)


def whole(*shape):
    return pl.BlockSpec(shape, lambda *_: (0,) * len(shape))


def main(lengths, codes, codebook, expand, latent_w, x, wd, we):
    return pl.pallas_call(
        main_kernel,
        grid_spec=pltpu.PrefetchScalarGridSpec(
            num_scalar_prefetch=1,
            grid=(STEPS,),
            in_specs=[
                whole(NB, 1, BLK),
                whole(CODES, LAT),
                whole(HID, LAT),
                whole(HID, LAT),
                pl.BlockSpec((ROWS, TILE), lambda i, s: (0, i)),
                pl.BlockSpec((HID, TILE), lambda i, s: (0, i)),
                pl.BlockSpec((TILE, HID), lambda i, s: (i, 0)),
            ],
            out_specs=[
                pl.BlockSpec((HID // 2, TILE), lambda i, s: (0, i)),
                pl.BlockSpec((HID // 2, TILE), lambda i, s: (0, i)),
                whole(ROWS, HID),
                whole(ROWS, LAT),
                whole(128, 8, LAT),
            ],
            scratch_shapes=[
                pltpu.VMEM((ROWS, LAT), BF),
                pltpu.VMEM((ROWS, HID), BF),
                pltpu.VMEM((HID, ROWS), BF),
                pltpu.VMEM((ROWS, 1), F32),
                pltpu.VMEM((ROWS, HID), F32),
                pltpu.VMEM((ROWS, HID), F32),
                pltpu.VMEM((HID, HID), BF),
            ],
        ),
        out_shape=[
            jax.ShapeDtypeStruct((HID // 2, FEAT), BF),
            jax.ShapeDtypeStruct((HID // 2, FEAT), BF),
            jax.ShapeDtypeStruct((ROWS, HID), BF),
            jax.ShapeDtypeStruct((ROWS, LAT), F32),
            jax.ShapeDtypeStruct((128, 8, LAT), BF),
        ],
        compiler_params=pltpu.CompilerParams(vmem_limit_bytes=60 << 20),
        cost_estimate=pl.CostEstimate(flops=20 * 10**9, bytes_accessed=24 << 20, transcendentals=0),
        name="forward_and_hidden_grads",
    )(lengths, codes, codebook, expand, latent_w, x, wd, we)


def pack(dest, lat, after):
    return pl.pallas_call(
        pack_kernel,
        grid_spec=pltpu.PrefetchScalarGridSpec(
            num_scalar_prefetch=1,
            grid=(1,),
            in_specs=[whole(ROWS, LAT), pl.BlockSpec(memory_space=pl.ANY)],
            out_specs=whole(PEERS, META, LAT),
            scratch_shapes=[pltpu.VMEM((PEERS, META, LAT), F32), pltpu.SMEM((PEERS,), jnp.int32)],
        ),
        out_shape=jax.ShapeDtypeStruct((PEERS, META, LAT), BF),
        compiler_params=pltpu.CompilerParams(vmem_limit_bytes=8 << 20),
        cost_estimate=pl.CostEstimate(flops=10**6, bytes_accessed=1 << 20, transcendentals=0),
        name="pack_latents",
    )(dest, lat, after)


def outer(x, bh, small):
    return pl.pallas_call(
        outer_kernel,
        grid=(4,),
        in_specs=[
            pl.BlockSpec((ROWS, FEAT // 4), lambda i: (0, i)),
            whole(ROWS, HID),
            whole(128, 8, LAT),
        ],
        out_specs=[whole(64, DROWS, LAT)] * 2,
        out_shape=[jax.ShapeDtypeStruct((64, DROWS, LAT), BF)] * 2,
        compiler_params=pltpu.CompilerParams(vmem_limit_bytes=48 << 20),
        cost_estimate=pl.CostEstimate(flops=44 * 10**8, bytes_accessed=13 << 20, transcendentals=0),
        name="encoder_grads",
    )(x, bh, small)


def join(e_own, e_arrived, d_own, d_arrived):
    return pl.pallas_call(
        join_kernel,
        out_shape=[jax.ShapeDtypeStruct((4, JROWS, LAT), F32)] + [jax.ShapeDtypeStruct((4, JROWS, LAT), BF)] * 3,
        scratch_shapes=[pltpu.VMEM((16, JROWS, LAT), F32)],
        compiler_params=pltpu.CompilerParams(vmem_limit_bytes=16 << 20),
        cost_estimate=pl.CostEstimate(flops=10**7, bytes_accessed=6 << 20, transcendentals=0),
        name="sum_first_exchange",
    )(e_own, *e_arrived, d_own, *d_arrived)


def last(own, arrived):
    return pl.pallas_call(
        last_kernel,
        out_shape=[
            jax.ShapeDtypeStruct((32, HID), F32),
            jax.ShapeDtypeStruct((4, LAT), F32),
            jax.ShapeDtypeStruct((4, LAT), F32),
            jax.ShapeDtypeStruct((4, FEAT), F32),
        ],
        compiler_params=pltpu.CompilerParams(vmem_limit_bytes=4 << 20),
        cost_estimate=pl.CostEstimate(flops=10**6, bytes_accessed=1 << 20, transcendentals=0),
        name="sum_last_exchange",
    )(own, *arrived)


def arrive(got):
    return pl.pallas_call(
        arrive_kernel,
        out_shape=jax.ShapeDtypeStruct((RB, BLK, LAT), F32),
        compiler_params=pltpu.CompilerParams(vmem_limit_bytes=4 << 20),
        cost_estimate=pl.CostEstimate(flops=10**6, bytes_accessed=1 << 20, transcendentals=0),
        name="place_latents",
    )(got)


def device(col, row, core, depth):
    return ((col * 4 + row) * 2 + core) * 4 + depth


def moves(change):
    return [
        (device(x, y, c, z), device(*change(x, y, c, z)))
        for x in range(4)
        for y in range(4)
        for c in range(2)
        for z in range(4)
    ]


BOTH = ("dp", "rep")


def flip(phase, by):
    def change(x, y, c, z):
        mask = 1 if (phase == 0) == (c == 0) else 3
        return x ^ (by // 2 * mask), y ^ (by % 2 * mask), c, z

    return moves(change)


def turn(by):
    return moves(lambda x, y, c, z: (x, y, c, (z + by) % 4))


def swap_cores(array):
    return lax.ppermute(array, BOTH, moves(lambda x, y, c, z: (x, y, 1 - c, z)))


def first_shares(keep, swap, size):
    def part(first):
        rows = slice(first * size, first * size + size)
        return keep[rows].astype(F32) + swap[rows].astype(F32)

    return part(0), [part(first).astype(BF) for first in (3, 2, 1)]


def per_device(
    frames,
    clip_lengths,
    block_dest,
    frame_codes,
    codebook,
    encoder_weight,
    latent_weight,
    expand_weight,
    decoder_weight,
):
    x = frames.reshape(ROWS, FEAT)
    send, keep, bh, lat, small = main(
        clip_lengths.reshape(4), frame_codes, codebook, expand_weight, latent_weight, x, decoder_weight, encoder_weight
    )
    d_swap = swap_cores(send)
    e_send, e_keep = outer(x, bh, small)
    e_swap = swap_cores(e_send)

    d_own, d_shares = first_shares(keep, d_swap, 64)
    d_arrived = [lax.ppermute(share, BOTH, flip(0, first)) for share, first in zip(d_shares, (3, 2, 1))]
    e_own, e_shares = first_shares(e_keep, e_swap, 16)
    e_arrived = [lax.ppermute(share, BOTH, flip(0, first)) for share, first in zip(e_shares, (3, 2, 1))]
    packed = pack(block_dest.reshape(2 * NB), lat, e_shares[0])
    got = lax.all_to_all(packed, "dp", 0, 0, tiled=True)

    own, *shares = join(e_own, e_arrived, d_own, d_arrived)
    shares, got = lax.optimization_barrier((shares, got))
    arrived = [lax.ppermute(shares[by - 1], BOTH, flip(1, by)) for by in (3, 2, 1)]
    latents = arrive(got)
    for piece in arrived:
        own = own + piece.astype(F32)
    arrived = [lax.ppermute(own[by : by + 1].astype(BF), BOTH, turn(by)) for by in (2, 3, 1)]
    grad_encoder, grad_latent, grad_expand, grad_decoder = last(own[:1], arrived)
    return latents[:, None], grad_encoder, grad_latent, grad_expand, grad_decoder


def solution(mesh):
    in_specs = (
        P("dp", "rep", None, None),
        P("dp", "rep", None),
        P("dp", "rep", None, None),
        P("dp", "rep", None),
        P(),
        P(),
        P(),
        P(),
        P(),
    )
    out_specs = (P("dp", "rep", None, None),) + (P(("dp", "rep"), None),) * 4
    return jax.shard_map(
        per_device, mesh=mesh, in_specs=in_specs, out_specs=out_specs, check_vma=False
    )
```

time: 133 us -> 106 us (0.80)
  starting transfers between devices: 38.5 us -> 28.8 us
  Pallas kernels: 50.1 us -> 42.2 us
  other arithmetic: 11 us -> 3.41 us
  local copies, waits for them, and re-layouts: 9.82 us -> 6.92 us
  waiting for transfers between devices: 22.1 us -> 23.8 us
    ppermute x20 -> x14, starting transfers between devices: 31.1 us -> 21.8 us  [the longest x6 9.3 us: per_device(): lax.ppermute(share, BOTH, flip(0, first))]
    add x4 -> x0, other arithmetic: 7.97 us -> none  [the longest x2 7.28 us: reduce_scatter(): total = keep.astype(F32) + got.astype(F32)]
    pallas_call x3 -> x5, Pallas kernels: 47.9 us -> 41 us  [the longest x1 28.4 us: main(): pl.pallas_call(main_kernel, grid_spec=pltpu.PrefetchScalarGridSpec(num_sc...]
    convert_element_type x0 -> x2, other arithmetic: none -> 3.26 us  [first_shares(): return (part(0), [part(first).astype(BF) for first in (3, 2, 1)])]
    another operation x4 -> x1, other arithmetic: 2.35 us -> 0.15 us
    slice x8 -> x2, local copies, waits for them, and re-layouts: 1.94 us -> 0.03 us  [the longest x1 0.02 us: per_device(): own[by:by + 1].astype(BF)]
    ppermute x20 -> x14, waiting for transfers between devices: 22.1 us -> 23.3 us  [the longest x6 12.8 us: per_device(): lax.ppermute(share, BOTH, flip(0, first))]
    unnamed x17 -> x19, local copies, waits for them, and re-layouts: 6.98 us -> 6.81 us
  transfers between devices with their start and end apart: 21 -> 15, of which waited for: 7 -> 9; matrix products, arithmetic and copies ran while one was open for 7% -> 3% of each run, Pallas kernels for 26% -> 12%
where the time goes in v2:
time: 106 us
  Pallas kernels  42.2 us (40%)
  starting transfers between devices  28.8 us (27%)
  waiting for transfers between devices  23.8 us (22%)
  local copies, waits for them, and re-layouts  6.92 us (7%)
  other arithmetic  3.41 us (3%)
    pallas_call x1, Pallas kernels, main(): pl.pallas_call(main_kernel, grid_spec=pltpu.PrefetchScalarGridSpec(num_sc...  28.4 us
    ppermute x6, waiting for transfers between devices, per_device(): lax.ppermute(share, BOTH, flip(0, first))  12.8 us
    ppermute x6, starting transfers between devices, per_device(): lax.ppermute(share, BOTH, flip(0, first))  9.3 us
    pallas_call x1, Pallas kernels, outer(): pl.pallas_call(outer_kernel, grid=(4,), in_specs=[pl.BlockSpec((ROWS, FEA...  7.47 us
    ppermute x3, waiting for transfers between devices, per_device(): lax.ppermute(shares[by - 1], BOTH, flip(1, by))  7.17 us
    all_to_all x1, starting transfers between devices, per_device(): got = lax.all_to_all(packed, 'dp', 0, 0, tiled=True)  7 us
    unnamed x19, local copies, waits for them, and re-layouts  6.81 us
    ppermute x3, starting transfers between devices, per_device(): lax.ppermute(own[by:by + 1].astype(BF), BOTH, turn(by))  5.99 us
  transfers between devices with their start and end apart: 15, of which 9 were waited for; matrix products, arithmetic and copies ran while one was open for 3% of the time, Pallas kernels for 12%

profile of v2, /device:TPU:0, one launch (start us, length us, event | category | flops | bytes accessed | tf_op | source)
XLA Modules:
  0.0 106.0 jit_solution(17867291126217498533)
XLA Ops:
  0.6 1.4 %copy.14.codes = s32[64,1,16]{2,1,0:T(1,128)} copy(s32[64,1,16]{0,2,1:T(8,128)} %param.12) | data formatting | bytes 8192 | tf_op args[3]
  2.0 28.4 %forward_and_hidden_grads.1 = (bf16[256,4096]{1,0:T(8,128)(2,1)}, bf16[256,4096]{1,0:T(8,128)(2,1)}, bf16[1024,512]{1,0:T(8,128)(2,1)}, f32[1024,128]{1,0:T(8,128)}, bf16[128,8,128]{2,1,0:T(8,128)(2,1)}) custom-call(s32[4]{0:T(128)} %bitcast.8, s32[64,1,16]{2,1,0:T(1,128)} %copy.14.codes, bf16[1024,128]{1,0:T(8,128)(2,1)} %codebook.1, ...), custom_call_target="tpu_custom_call" | custom-call | flops 20000000000 | bytes 25165824 | tf_op jit(solution)/shard_map/forward_and_hidden_grads/pallas_call | solution.py:239
  30.4 0.1 collective-permute-start.4
  30.5 1.2 %copy-done.5 = bf16[1024,512]{1,0:T(8,128)(2,1)S(1)} copy-done((bf16[1024,512]{1,0:T(8,128)(2,1)S(1)}, bf16[1024,512]{1,0:T(8,128)(2,1)}, u32[]{:S(2)}) %copy-start.5) | copy-done | bytes 1048600
  31.7 0.9 copy-done.6
  32.7 7.5 %encoder_grads.1 = (bf16[64,136,128]{2,1,0:T(8,128)(2,1)S(1)}, bf16[64,136,128]{2,1,0:T(8,128)(2,1)S(1)}) custom-call(bf16[1024,4096]{1,0:T(8,128)(2,1)} %bitcast.7, bf16[1024,512]{1,0:T(8,128)(2,1)S(1)} %copy-done.5, bf16[128,8,128]{2,1,0:T(8,128)(2,1)S(1)} %copy-done.6), custom_call_target="tpu_custom_call" | custom-call | flops 4400000000 | bytes 13631488 | tf_op jit(solution)/shard_map/encoder_grads/pallas_call | solution.py:301
  40.1 0.6 collective-permute-start
  40.7 0.0 collective-permute-done.4
  40.7 0.0 copy-done.7
  40.7 1.7 %add_convert_fusion.3 = (bf16[64,4096]{1,0:T(8,128)(2,1)S(1)}, bf16[64,4096]{1,0:T(8,128)(2,1)}, bf16[64,4096]{1,0:T(8,128)(2,1)}, f32[64,4096]{1,0:T(8,128)S(1)}) fusion(bf16[256,4096]{1,0:T(8,128)(2,1)S(1)} %collective-permute-done.4, bf16[256,4096]{1,0:T(8,128)(2,1)S(1)} %copy-done.7), kind=kLoop, calls=%fused_computation.4 | loop fusion | flops 3932160 | bytes 6815744 | tf_op jit(solution)/shard_map/convert_element_type | solution.py:391
  42.4 1.7 %collective-permute-start.7 = (bf16[64,4096]{1,0:T(8,128)(2,1)S(1)}, bf16[64,4096]{1,0:T(8,128)(2,1)S(1)}, u32[]{:S(2)}, u32[]{:S(2)}) collective-permute-start(bf16[64,4096]{1,0:T(8,128)(2,1)S(1)} %get-tuple-element.54), channel_id=1, source_target_pairs={{0,8},{1,9},{2,10},{3,11},{4,28},{5,29},{6,30},{7,31},{8,0},{9,1},... | collective-permute-start | bytes 1572872 | tf_op jit(solution)/shard_map/ppermute | solution.py:414
  44.1 0.6 collective-permute-done
  44.7 1.5 %add_convert_fusion = (bf16[16,136,128]{2,1,0:T(8,128)(2,1)}, bf16[16,136,128]{2,1,0:T(8,128)(2,1)}, bf16[16,136,128]{2,1,0:T(8,128)(2,1)S(1)}, f32[16,136,128]{2,1,0:T(8,128)S(1)}) fusion(bf16[64,136,128]{2,1,0:T(8,128)(2,1)S(1)} %collective-permute-done, bf16[64,136,128]{2,1,0:T(8,128)(2,1)S(1)} %get-tuple-element.26), kind=kLoop, calls=%fused_computation | loop fusion | flops 4177920 | bytes 7241728 | tf_op jit(solution)/shard_map/convert_element_type | solution.py:391
  46.2 1.7 %collective-permute-start.3 = (bf16[16,136,128]{2,1,0:T(8,128)(2,1)}, bf16[16,136,128]{2,1,0:T(8,128)(2,1)}, u32[]{:S(2)}, u32[]{:S(2)}) collective-permute-start(bf16[16,136,128]{2,1,0:T(8,128)(2,1)} %get-tuple-element.50), channel_id=1, source_target_pairs={{0,8},{1,9},{2,10},{3,11},{4,28},{5,29},{6,30},{7,31},{8,0},{9,1},... | collective-permute-start | bytes 1671176 | tf_op jit(solution)/shard_map/ppermute | solution.py:416
  47.9 1.5 %collective-permute-start.2 = (bf16[16,136,128]{2,1,0:T(8,128)(2,1)}, bf16[16,136,128]{2,1,0:T(8,128)(2,1)}, u32[]{:S(2)}, u32[]{:S(2)}) collective-permute-start(bf16[16,136,128]{2,1,0:T(8,128)(2,1)} %get-tuple-element.51), channel_id=1, source_target_pairs={{0,32},{1,33},{2,34},{3,35},{4,100},{5,101},{6,102},{7,103},{8,40}... | collective-permute-start | bytes 1671176 | tf_op jit(solution)/shard_map/ppermute | solution.py:416
  49.4 0.3 collective-permute-start.1
  49.7 1.6 %collective-permute-start.6 = (bf16[64,4096]{1,0:T(8,128)(2,1)}, bf16[64,4096]{1,0:T(8,128)(2,1)}, u32[]{:S(2)}, u32[]{:S(2)}) collective-permute-start(bf16[64,4096]{1,0:T(8,128)(2,1)} %get-tuple-element.55), channel_id=1, source_target_pairs={{0,32},{1,33},{2,34},{3,35},{4,100},{5,101},{6,102},{7,103},{8,40}... | collective-permute-start | bytes 1572872 | tf_op jit(solution)/shard_map/ppermute | solution.py:414
  51.3 0.3 collective-permute-done.7.d1
  51.6 0.8 copy-done.1
  52.4 2.6 %collective-permute-start.5 = (bf16[64,4096]{1,0:T(8,128)(2,1)}, bf16[64,4096]{1,0:T(8,128)(2,1)}, u32[]{:S(2)}, u32[]{:S(2)}) collective-permute-start(bf16[64,4096]{1,0:T(8,128)(2,1)} %get-tuple-element.56), channel_id=1, source_target_pairs={{0,40},{1,41},{2,42},{3,43},{4,124},{5,125},{6,126},{7,127},{8,32}... | collective-permute-start | bytes 1572872 | tf_op jit(solution)/shard_map/ppermute | solution.py:414
  55.0 0.1 reshape.21.dest
  55.1 2.3 %pack_latents.1 = bf16[32,40,128]{2,1,0:T(8,128)(2,1)} custom-call(s32[128]{0:T(128)S(1)} %reshape.21.dest, f32[1024,128]{1,0:T(8,128)S(1)} %copy-done, bf16[16,136,128]{2,1,0:T(8,128)(2,1)S(1)} %get-tuple-element.52._), custom_call_target="tpu_custom_call" | custom-call | flops 1000000 | bytes 1048576 | tf_op jit(solution)/shard_map/pack_latents/pallas_call | solution.py:284
  57.4 7.0 %all-to-all-start = ((bf16[32,40,128]{2,1,0:T(8,128)(2,1)}), bf16[32,40,128]{2,1,0:T(8,128)(2,1)S(1)}, u32[]{:S(2)}, u32[]{:S(2)}) async-start(bf16[32,40,128]{2,1,0:T(8,128)(2,1)} %pack_latents.1), calls=%async_computation | async-start | bytes 655360 | tf_op jit(solution)/shard_map/all_to_all | solution.py:418
  64.4 6.7 %collective-permute-done.6.d2 = bf16[64,4096]{1,0:T(8,128)(2,1)} collective-permute-done((bf16[64,4096]{1,0:T(8,128)(2,1)}, bf16[64,4096]{1,0:T(8,128)(2,1)}, u32[]{:S(2)}, u32[]{:S(2)}) %collective-permute-start.6) | collective-permute-done | bytes 524320 | tf_op jit(solution)/shard_map/ppermute | solution.py:414
  71.1 5.7 %collective-permute-done.5.d3 = bf16[64,4096]{1,0:T(8,128)(2,1)} collective-permute-done((bf16[64,4096]{1,0:T(8,128)(2,1)}, bf16[64,4096]{1,0:T(8,128)(2,1)}, u32[]{:S(2)}, u32[]{:S(2)}) %collective-permute-start.5) | collective-permute-done | bytes 524320 | tf_op jit(solution)/shard_map/ppermute | solution.py:414
  76.8 0.0 collective-permute-done.3.e1
  76.8 0.0 collective-permute-done.2.e2
  76.9 0.0 collective-permute-done.1.e3
  76.9 1.0 copy-done.2
  77.9 2.2 %sum_first_exchange.1 = (f32[4,264,128]{2,1,0:T(8,128)S(1)}, bf16[4,264,128]{2,1,0:T(8,128)(2,1)S(1)}, bf16[4,264,128]{2,1,0:T(8,128)(2,1)S(1)}, bf16[4,264,128]{2,1,0:T(8,128)(2,1)S(1)}) custom-call(f32[16,136,128]{2,1,0:T(8,128)S(1)} %get-tuple-element.53.own_e, bf16[16,136,128]{2,1,0:T(8,128)(2,1)} %collective-permute-done.1.e3, ...), custom_call_target="tpu_custom_call" | custom-call | flops 10000000 | bytes 6291456 | tf_op jit(solution)/shard_map/sum_first_exchange/pallas_call | solution.py:318
  80.1 0.7 copy-done.3
  80.8 0.7 copy-done.4
  81.5 0.5 all-to-all-done.got
  82.0 4.8 %collective-permute-start.8 = (bf16[4,264,128]{2,1,0:T(8,128)(2,1)}, bf16[4,264,128]{2,1,0:T(8,128)(2,1)S(1)}, u32[]{:S(2)}, u32[]{:S(2)}) collective-permute-start(bf16[4,264,128]{2,1,0:T(8,128)(2,1)} %copy-done.4), channel_id=1, source_target_pairs={{0,120},{1,121},{2,122},{3,123},{4,44},{5,45},{6,46},{7,47},{8,112... | collective-permute-start | bytes 811016 | tf_op jit(solution)/shard_map/ppermute | solution.py:422
  86.9 0.6 collective-permute-start.9
  87.5 0.5 collective-permute-start.10
  88.0 4.1 %collective-permute-done.8 = bf16[4,264,128]{2,1,0:T(8,128)(2,1)S(1)} collective-permute-done((bf16[4,264,128]{2,1,0:T(8,128)(2,1)}, bf16[4,264,128]{2,1,0:T(8,128)(2,1)S(1)}, u32[]{:S(2)}, u32[]{:S(2)}) %collective-permute-start.8) | collective-permute-done | bytes 270368 | tf_op jit(solution)/shard_map/ppermute | solution.py:422
  92.0 3.0 %collective-permute-done.9 = bf16[4,264,128]{2,1,0:T(8,128)(2,1)S(1)} collective-permute-done((bf16[4,264,128]{2,1,0:T(8,128)(2,1)}, bf16[4,264,128]{2,1,0:T(8,128)(2,1)S(1)}, u32[]{:S(2)}, u32[]{:S(2)}) %collective-permute-start.9) | collective-permute-done | bytes 270368 | tf_op jit(solution)/shard_map/ppermute | solution.py:422
  95.0 0.1 collective-permute-done.10
  95.1 0.1 fusion
  95.3 2.0 %collective-permute-start.13 = (bf16[1,264,128]{2,1,0:T(8,128)(2,1)S(1)}, bf16[1,264,128]{2,1,0:T(8,128)(2,1)S(1)}, u32[]{:S(2)}, u32[]{:S(2)}) collective-permute-start(bf16[1,264,128]{2,1,0:T(8,128)(2,1)S(1)} %get-tuple-element.58), channel_id=1, source_target_pairs={{0,1},{1,2},{2,3},{3,0},{4,5},{5,6},{6,7},{7,4},{8,9},{9,10},{10,1... | collective-permute-start | bytes 202760 | tf_op jit(solution)/shard_map/ppermute | solution.py:426
  97.3 2.2 %collective-permute-start.12 = (bf16[1,264,128]{2,1,0:T(8,128)(2,1)S(1)}, bf16[1,264,128]{2,1,0:T(8,128)(2,1)S(1)}, u32[]{:S(2)}, u32[]{:S(2)}) collective-permute-start(bf16[1,264,128]{2,1,0:T(8,128)(2,1)S(1)} %get-tuple-element.59), channel_id=1, source_target_pairs={{0,3},{1,0},{2,1},{3,2},{4,7},{5,4},{6,5},{7,6},{8,11},{9,8},{10,9... | collective-permute-start | bytes 202760 | tf_op jit(solution)/shard_map/ppermute | solution.py:426
  99.5 1.8 %collective-permute-start.11 = (bf16[1,264,128]{2,1,0:T(8,128)(2,1)S(1)}, bf16[1,264,128]{2,1,0:T(8,128)(2,1)S(1)}, u32[]{:S(2)}, u32[]{:S(2)}) collective-permute-start(bf16[1,264,128]{2,1,0:T(8,128)(2,1)S(1)} %get-tuple-element.60), channel_id=1, source_target_pairs={{0,2},{1,3},{2,0},{3,1},{4,6},{5,7},{6,4},{7,5},{8,10},{9,11},{10,... | collective-permute-start | bytes 202760 | tf_op jit(solution)/shard_map/ppermute | solution.py:426
  101.3 1.2 %place_latents.1 = f32[32,16,128]{2,1,0:T(8,128)} custom-call(bf16[32,40,128]{2,1,0:T(8,128)(2,1)S(1)} %all-to-all-done.got), custom_call_target="tpu_custom_call" | custom-call | flops 1000000 | bytes 1048576 | tf_op jit(solution)/shard_map/place_latents/pallas_call | solution.py:344
  102.5 0.0 collective-permute-done.13.a1
  102.5 0.0 collective-permute-done.12.a2
  102.5 2.8 %collective-permute-done.11.a3 = bf16[1,264,128]{2,1,0:T(8,128)(2,1)S(1)} collective-permute-done((bf16[1,264,128]{2,1,0:T(8,128)(2,1)S(1)}, bf16[1,264,128]{2,1,0:T(8,128)(2,1)S(1)}, u32[]{:S(2)}, u32[]{:S(2)}) %collective-permute-start.11) | collective-permute-done | bytes 67616 | tf_op jit(solution)/shard_map/ppermute | solution.py:426
  105.3 0.7 sum_last_exchange.1
  (13 shorter events, 0.0 us)
Async XLA Ops:
  30.4 10.3 %collective-permute-start.4 = (bf16[256,4096]{1,0:T(8,128)(2,1)}, bf16[256,4096]{1,0:T(8,128)(2,1)S(1)}, u32[]{:S(2)}, u32[]{:S(2)}) collective-permute-start(bf16[256,4096]{1,0:T(8,128)(2,1)} %get-tuple-element.29), channel_id=1, source_target_pairs={{0,4},{1,5},{2,6},{3,7},{4,0},{5,1},{6,2},{7,3},{8,12},{9,13},{10,... | collective-permute-start | bytes 6291464 | tf_op jit(solution)/shard_map/ppermute | solution.py:383
  30.5 1.2 %copy-start.5 = (bf16[1024,512]{1,0:T(8,128)(2,1)S(1)}, bf16[1024,512]{1,0:T(8,128)(2,1)}, u32[]{:S(2)}) copy-start(bf16[1024,512]{1,0:T(8,128)(2,1)} %get-tuple-element.24.bh) | copy-start | bytes 3145732
  31.7 0.9 copy-start.6
  32.7 8.0 %copy-start.7 = (bf16[256,4096]{1,0:T(8,128)(2,1)S(1)}, bf16[256,4096]{1,0:T(8,128)(2,1)}, u32[]{:S(2)}) copy-start(bf16[256,4096]{1,0:T(8,128)(2,1)} %get-tuple-element.28) | copy-start | bytes 6291460
  40.1 4.5 %collective-permute-start = (bf16[64,136,128]{2,1,0:T(8,128)(2,1)S(1)}, bf16[64,136,128]{2,1,0:T(8,128)(2,1)S(1)}, u32[]{:S(2)}, u32[]{:S(2)}) collective-permute-start(bf16[64,136,128]{2,1,0:T(8,128)(2,1)S(1)} %get-tuple-element.27), channel_id=1, source_target_pairs={{0,4},{1,5},{2,6},{3,7},{4,0},{5,1},{6,2},{7,3},{8,12},{9,13},{10,... | collective-permute-start | bytes 6684680 | tf_op jit(solution)/shard_map/ppermute | solution.py:383
  42.4 9.2 %collective-permute-start.7 = (bf16[64,4096]{1,0:T(8,128)(2,1)S(1)}, bf16[64,4096]{1,0:T(8,128)(2,1)S(1)}, u32[]{:S(2)}, u32[]{:S(2)}) collective-permute-start(bf16[64,4096]{1,0:T(8,128)(2,1)S(1)} %get-tuple-element.54), channel_id=1, source_target_pairs={{0,8},{1,9},{2,10},{3,11},{4,28},{5,29},{6,30},{7,31},{8,0},{9,1},... | collective-permute-start | bytes 1572872 | tf_op jit(solution)/shard_map/ppermute | solution.py:414
  44.7 10.3 %copy-start.8 = (s32[1,1,2,64]{3,2,1,0:T(2,128)S(1)}, s32[1,1,2,64]{3,2,1,0:T(2,128)}, u32[]{:S(2)}) copy-start(s32[1,1,2,64]{3,2,1,0:T(2,128)} %param.11) | copy-start | bytes 1540
  44.7 10.4 %copy-start = (f32[1024,128]{1,0:T(8,128)S(1)}, f32[1024,128]{1,0:T(8,128)}, u32[]{:S(2)}) copy-start(f32[1024,128]{1,0:T(8,128)} %get-tuple-element.33.lat) | copy-start | bytes 1572868
  46.2 30.6 %collective-permute-start.3 = (bf16[16,136,128]{2,1,0:T(8,128)(2,1)}, bf16[16,136,128]{2,1,0:T(8,128)(2,1)}, u32[]{:S(2)}, u32[]{:S(2)}) collective-permute-start(bf16[16,136,128]{2,1,0:T(8,128)(2,1)} %get-tuple-element.50), channel_id=1, source_target_pairs={{0,8},{1,9},{2,10},{3,11},{4,28},{5,29},{6,30},{7,31},{8,0},{9,1},... | collective-permute-start | bytes 1671176 | tf_op jit(solution)/shard_map/ppermute | solution.py:416
  47.9 29.0 %collective-permute-start.2 = (bf16[16,136,128]{2,1,0:T(8,128)(2,1)}, bf16[16,136,128]{2,1,0:T(8,128)(2,1)}, u32[]{:S(2)}, u32[]{:S(2)}) collective-permute-start(bf16[16,136,128]{2,1,0:T(8,128)(2,1)} %get-tuple-element.51), channel_id=1, source_target_pairs={{0,32},{1,33},{2,34},{3,35},{4,100},{5,101},{6,102},{7,103},{8,40}... | collective-permute-start | bytes 1671176 | tf_op jit(solution)/shard_map/ppermute | solution.py:416
  49.4 27.5 %collective-permute-start.1 = (bf16[16,136,128]{2,1,0:T(8,128)(2,1)S(1)}, bf16[16,136,128]{2,1,0:T(8,128)(2,1)}, u32[]{:S(2)}, u32[]{:S(2)}) collective-permute-start(bf16[16,136,128]{2,1,0:T(8,128)(2,1)S(1)} %get-tuple-element.52._), channel_id=1, source_target_pairs={{0,40},{1,41},{2,42},{3,43},{4,124},{5,125},{6,126},{7,127},{8,32}... | collective-permute-start | bytes 1671176 | tf_op jit(solution)/shard_map/ppermute | solution.py:416
  49.7 21.4 %collective-permute-start.6 = (bf16[64,4096]{1,0:T(8,128)(2,1)}, bf16[64,4096]{1,0:T(8,128)(2,1)}, u32[]{:S(2)}, u32[]{:S(2)}) collective-permute-start(bf16[64,4096]{1,0:T(8,128)(2,1)} %get-tuple-element.55), channel_id=1, source_target_pairs={{0,32},{1,33},{2,34},{3,35},{4,100},{5,101},{6,102},{7,103},{8,40}... | collective-permute-start | bytes 1572872 | tf_op jit(solution)/shard_map/ppermute | solution.py:414
  51.6 0.8 copy-start.1
  52.4 24.5 %collective-permute-start.5 = (bf16[64,4096]{1,0:T(8,128)(2,1)}, bf16[64,4096]{1,0:T(8,128)(2,1)}, u32[]{:S(2)}, u32[]{:S(2)}) collective-permute-start(bf16[64,4096]{1,0:T(8,128)(2,1)} %get-tuple-element.56), channel_id=1, source_target_pairs={{0,40},{1,41},{2,42},{3,43},{4,124},{5,125},{6,126},{7,127},{8,32}... | collective-permute-start | bytes 1572872 | tf_op jit(solution)/shard_map/ppermute | solution.py:414
  57.4 24.7 %all-to-all-start = ((bf16[32,40,128]{2,1,0:T(8,128)(2,1)}), bf16[32,40,128]{2,1,0:T(8,128)(2,1)S(1)}, u32[]{:S(2)}, u32[]{:S(2)}) async-start(bf16[32,40,128]{2,1,0:T(8,128)(2,1)} %pack_latents.1), calls=%async_computation | async-start | bytes 655360 | tf_op jit(solution)/shard_map/all_to_all | solution.py:418
  76.9 1.0 copy-start.2
  80.1 0.7 copy-start.3
  80.8 0.7 copy-start.4
  82.0 10.0 %collective-permute-start.8 = (bf16[4,264,128]{2,1,0:T(8,128)(2,1)}, bf16[4,264,128]{2,1,0:T(8,128)(2,1)S(1)}, u32[]{:S(2)}, u32[]{:S(2)}) collective-permute-start(bf16[4,264,128]{2,1,0:T(8,128)(2,1)} %copy-done.4), channel_id=1, source_target_pairs={{0,120},{1,121},{2,122},{3,123},{4,44},{5,45},{6,46},{7,47},{8,112... | collective-permute-start | bytes 811016 | tf_op jit(solution)/shard_map/ppermute | solution.py:422
  86.9 8.1 %collective-permute-start.9 = (bf16[4,264,128]{2,1,0:T(8,128)(2,1)}, bf16[4,264,128]{2,1,0:T(8,128)(2,1)S(1)}, u32[]{:S(2)}, u32[]{:S(2)}) collective-permute-start(bf16[4,264,128]{2,1,0:T(8,128)(2,1)} %copy-done.3), channel_id=1, source_target_pairs={{0,96},{1,97},{2,98},{3,99},{4,36},{5,37},{6,38},{7,39},{8,104},{9... | collective-permute-start | bytes 811016 | tf_op jit(solution)/shard_map/ppermute | solution.py:422
  87.5 7.7 %collective-permute-start.10 = (bf16[4,264,128]{2,1,0:T(8,128)(2,1)S(1)}, bf16[4,264,128]{2,1,0:T(8,128)(2,1)S(1)}, u32[]{:S(2)}, u32[]{:S(2)}) collective-permute-start(bf16[4,264,128]{2,1,0:T(8,128)(2,1)S(1)} %get-tuple-element.38), channel_id=1, source_target_pairs={{0,24},{1,25},{2,26},{3,27},{4,12},{5,13},{6,14},{7,15},{8,16},{9,... | collective-permute-start | bytes 811016 | tf_op jit(solution)/shard_map/ppermute | solution.py:422
  95.3 7.2 %collective-permute-start.13 = (bf16[1,264,128]{2,1,0:T(8,128)(2,1)S(1)}, bf16[1,264,128]{2,1,0:T(8,128)(2,1)S(1)}, u32[]{:S(2)}, u32[]{:S(2)}) collective-permute-start(bf16[1,264,128]{2,1,0:T(8,128)(2,1)S(1)} %get-tuple-element.58), channel_id=1, source_target_pairs={{0,1},{1,2},{2,3},{3,0},{4,5},{5,6},{6,7},{7,4},{8,9},{9,10},{10,1... | collective-permute-start | bytes 202760 | tf_op jit(solution)/shard_map/ppermute | solution.py:426
  97.3 5.2 %collective-permute-start.12 = (bf16[1,264,128]{2,1,0:T(8,128)(2,1)S(1)}, bf16[1,264,128]{2,1,0:T(8,128)(2,1)S(1)}, u32[]{:S(2)}, u32[]{:S(2)}) collective-permute-start(bf16[1,264,128]{2,1,0:T(8,128)(2,1)S(1)} %get-tuple-element.59), channel_id=1, source_target_pairs={{0,3},{1,0},{2,1},{3,2},{4,7},{5,4},{6,5},{7,6},{8,11},{9,8},{10,9... | collective-permute-start | bytes 202760 | tf_op jit(solution)/shard_map/ppermute | solution.py:426
  99.5 5.8 %collective-permute-start.11 = (bf16[1,264,128]{2,1,0:T(8,128)(2,1)S(1)}, bf16[1,264,128]{2,1,0:T(8,128)(2,1)S(1)}, u32[]{:S(2)}, u32[]{:S(2)}) collective-permute-start(bf16[1,264,128]{2,1,0:T(8,128)(2,1)S(1)} %get-tuple-element.60), channel_id=1, source_target_pairs={{0,2},{1,3},{2,0},{3,1},{4,6},{5,7},{6,4},{7,5},{8,10},{9,11},{10,... | collective-permute-start | bytes 202760 | tf_op jit(solution)/shard_map/ppermute | solution.py:426

commit v3 on v2

--- a/solution.py
+++ b/solution.py
@@ -14,7 +14,8 @@
 HID = 512
 LAT = 128
 CODES = 1024
-ROWS = NB * BLK
+USED = 60
+ROWS = USED * BLK
 PEERS = 32
 META = 2 * BLK + 8
 DROWS = 136
@@ -67,21 +68,32 @@
     return ((col * 4 + row) * 2 + core) * 4 + ((scal[Z] + rank) & 3)
 
 
+def hidden_of(row, scal):
+    rank = row >> 2
+    core = (1 - (rank >> 6)) ^ scal[C]
+    near = 1 + 2 * core
+    far = 3 - 2 * core
+    depth = scal[Z] ^ ((rank >> 5 & 1) * near) ^ ((rank >> 4 & 1) * far)
+    col = scal[X] ^ ((rank >> 3 & 1) * far) ^ ((rank >> 1 & 1) * near)
+    line = scal[Y] ^ ((rank >> 2 & 1) * far) ^ ((rank & 1) * near)
+    return ((((col * 4 + line) * 2 + core) * 4 + depth) << 2) + (row & 3)
+
+
 def main_kernel(
     lengths, codes, codebook, expand, latent_w, x, wd, we,
-    send, keep, bh, lat, small,
-    q_s, decoded, dec_t, w2, back_acc, pre_acc, order,
+    send, keep, bh, lat, small_keep, e_send,
+    q_s, decoded, dec_t, w2, back_acc, pre_acc, order, frames, small,
 ):
     step = pl.program_id(0)
     scal = place_of_device()
 
     @pl.when(step == 0)
     def _():
-        by_slot = codes[:, 0, :]
+        by_slot = codes[:USED, 0, :]
         spread = (iota((BLK, ROWS), 1) & (BLK - 1) == iota((BLK, ROWS), 0)).astype(BF)
         high = dot((by_slot >> 5).astype(F32).astype(BF), spread, 1, 0)
         low = dot((by_slot & 31).astype(F32).astype(BF), spread, 1, 0)
-        mine = iota((NB, ROWS), 1) >> 4 == iota((NB, ROWS), 0)
+        mine = iota((USED, ROWS), 1) >> 4 == iota((USED, ROWS), 0)
         row = jnp.sum(jnp.where(mine, high * 32.0 + low, 0.0), axis=0, keepdims=True).astype(jnp.int32)
         hot = (iota((CODES, ROWS), 0) == row).astype(BF)
         q_t = dot(codebook[...], hot, 0, 0).astype(BF)
@@ -89,23 +101,26 @@
         q_s[...] = q
         pre = dot(q, expand[...], 1, 1)
         decoded[...] = jnp.where(pre > 0, pre, slope_of(pre) - 1.0).astype(BF)
-        source = iota((HID, 1), 0)
-        source = dest_of(source >> 2, scal) * 4 + (source & 3)
-        order[...] = (iota((HID, HID), 1) == source).astype(BF)
-        moved = dot(order[...], expand[...], 1, 0).astype(BF)
+        row = iota((HID, 1), 0)
+        order[...] = (iota((HID, HID), 1) == dest_of(row >> 2, scal) * 4 + (row & 3)).astype(BF)
+        moved = (iota((HID, HID), 1) == hidden_of(row, scal)).astype(BF)
+        moved = dot(moved, expand[...], 1, 0).astype(BF)
         pre = dot(moved, q_t, 1, 0)
         dec_t[...] = jnp.where(pre > 0, pre, slope_of(pre) - 1.0).astype(BF)
         w2[...] = double_weight(lengths)
         back_acc[...] = jnp.zeros_like(back_acc)
         pre_acc[...] = jnp.zeros_like(pre_acc)
 
-    restored = dot(decoded[...], wd[...], 1, 0)
-    pre_acc[...] += dot(x[...], we[...], 1, 0)
-    grad = (w2[...] * (restored - x[...].astype(F32))).astype(BF)
-    out = dot(dec_t[...], grad, 1, 0)
-    send[...] = out[: HID // 2].astype(BF)
-    keep[...] = out[HID // 2 :].astype(BF)
-    back_acc[...] += dot(grad, wd[...], 1, 1)
+    @pl.when(step < STEPS)
+    def _():
+        frames[:, pl.ds(pl.multiple_of(step * TILE, TILE), TILE)] = x[...]
+        restored = dot(decoded[...], wd[...], 1, 0)
+        pre_acc[...] += dot(x[...], we[...], 1, 0)
+        grad = (w2[...] * (restored - x[...].astype(F32))).astype(BF)
+        out = dot(dec_t[...], grad, 1, 0)
+        send[...] = out[: HID // 2].astype(BF)
+        keep[...] = out[HID // 2 :].astype(BF)
+        back_acc[...] += dot(grad, wd[...], 1, 1)
 
     @pl.when(step == STEPS - 1)
     def _():
@@ -128,6 +143,23 @@
             left, right = grad_latent[8 * pair : 8 * pair + 8], grad_expand[8 * pair : 8 * pair + 8]
             small[2 * pair] = jnp.where(upper, left, pltpu.roll(right, 4, 0)).astype(BF)
             small[2 * pair + 1] = jnp.where(upper, pltpu.roll(left, 4, 0), right).astype(BF)
+        small_keep[...] = small[64:]
+
+    @pl.when(step >= STEPS)
+    def _():
+        first = step - STEPS
+        wide = [
+            frames[:, pl.ds(pl.multiple_of(dest_of(first * 16 + second * 4, scal) // 4 * 128, 128), 128)]
+            for second in range(4)
+        ]
+        grad = dot(jnp.concatenate(wide, axis=1), bh[...], 0, 0).astype(BF)
+        for second in range(4):
+            for depth in range(4):
+                spot = second * 4 + ((depth + 4 - scal[Z]) & 3)
+                top = 128 * second + 32 * depth
+                for part in range(4):
+                    e_send[spot, 32 * part : 32 * part + 32, :] = grad[top : top + 32, 128 * part : 128 * part + 128]
+        e_send[:, 128:DROWS, :] = small[pl.ds(first * 16, 16)]
 
 
 def pack_kernel(dest, lat, _, packed, spread, count):
@@ -151,41 +183,39 @@
 
         return 0
 
-    lax.fori_loop(0, NB, place, 0)
+    lax.fori_loop(0, USED, place, 0)
     packed[...] = spread[...].astype(BF)
 
 
-def outer_kernel(x, bh, small, send, keep):
+def outer_kernel(x, bh, small, out):
+    step = pl.program_id(0)
     scal = place_of_device()
-    step = pl.program_id(0)
-    for half, out in ((0, send), (1, keep)):
-        core = scal[C] if half else 1 - scal[C]
-        near = 1 + 2 * core
-        wide = [x[:, pl.ds(pl.multiple_of(256 * row + 128 * core, 128), 128)] for row in range(4)]
-        grad = dot(jnp.concatenate(wide, axis=1), bh[...], 0, 0).astype(BF)
-
-        def bits(relative):
-            middle = relative == 2
-            first = (middle | (relative == near)).astype(jnp.int32)
-            return first, (middle | (relative == 4 - near)).astype(jnp.int32)
-
-        col_first, col_second = bits(step ^ scal[X])
-        for row in range(4):
-            row_first, row_second = bits(row ^ scal[Y])
-            base = ((col_first * 2 + row_first) * 4 + col_second * 2 + row_second) * 4
-            for depth in range(4):
-                spot = base + ((depth + 4 - scal[Z]) & 3)
-                top = 128 * row + 32 * depth
-                for part in range(4):
-                    out[spot, 32 * part : 32 * part + 32, :] = grad[top : top + 32, 128 * part : 128 * part + 128]
+    core = scal[C]
+    near = 1 + 2 * core
+    wide = [x[:, pl.ds(pl.multiple_of(256 * row + 128 * core, 128), 128)] for row in range(4)]
+    grad = dot(jnp.concatenate(wide, axis=1), bh[...], 0, 0).astype(BF)
+
+    def bits(relative):
+        middle = relative == 2
+        first = (middle | (relative == near)).astype(jnp.int32)
+        return first, (middle | (relative == 4 - near)).astype(jnp.int32)
+
+    col_first, col_second = bits(step ^ scal[X])
+    for row in range(4):
+        row_first, row_second = bits(row ^ scal[Y])
+        base = ((col_first * 2 + row_first) * 4 + col_second * 2 + row_second) * 4
+        for depth in range(4):
+            spot = base + ((depth + 4 - scal[Z]) & 3)
+            top = 128 * row + 32 * depth
+            for part in range(4):
+                out[spot, 32 * part : 32 * part + 32, :] = grad[top : top + 32, 128 * part : 128 * part + 128]
 
     @pl.when(step == 3)
     def _():
-        send[:, 128:DROWS, :] = small[:64]
-        keep[:, 128:DROWS, :] = small[64:]
-
-
-def join_kernel(own_e, e3, e2, e1, own_d, d3, d2, d1, own, s1, s2, s3, acc):
+        out[:, 128:DROWS, :] = small[...]
+
+
+def join_kernel(own_e, e3, e2, e1, own_d, d_far, own, s1, s2, s3, acc):
     total = own_e[...]
     for piece in (e3, e2, e1):
         total = total + piece[...].astype(F32)
@@ -193,9 +223,7 @@
     upper = iota((8, LAT), 0) < 4
     for pair in range(8):
         rows = slice(8 * pair, 8 * pair + 8)
-        total = own_d[rows, :]
-        for piece in (d3, d2, d1):
-            total = total + piece[rows, :].astype(F32)
+        total = own_d[rows, :] + d_far[rows, :].astype(F32)
         for cols in range(16):
             left = total[:, 256 * cols : 256 * cols + 128]
             right = total[:, 256 * cols + 128 : 256 * cols + 256]
@@ -208,17 +236,20 @@
     s3[...] = acc[12:16].astype(BF)
 
 
-def last_kernel(own, a3, a2, a1, enc, lat, exp, dec):
-    total = own[0]
-    for piece in (a3, a2, a1):
+def last_kernel(own, e3, e2, e1, d3, d2, d1, enc, lat, exp, dec):
+    total = own[0, :DROWS, :]
+    for piece in (e3, e2, e1):
         total = total + piece[0].astype(F32)
     for part in range(4):
         enc[:, 128 * part : 128 * part + 128] = total[32 * part : 32 * part + 32]
     tail = total[128:DROWS]
     lat[...] = tail[:4]
     exp[...] = tail[4:]
+    total = own[0, DROWS:, :]
+    for piece in (d3, d2, d1):
+        total = total + piece[0].astype(F32)
     for cols in range(32):
-        dec[:, 128 * cols : 128 * cols + 128] = total[DROWS + 4 * cols : DROWS + 4 * cols + 4]
+        dec[:, 128 * cols : 128 * cols + 128] = total[4 * cols : 4 * cols + 4]
 
 
 def arrive_kernel(got, out):
@@ -236,26 +267,28 @@
 
 
 def main(lengths, codes, codebook, expand, latent_w, x, wd, we):
+    columns = lambda i, s: (0, jnp.minimum(i, STEPS - 1))
     return pl.pallas_call(
         main_kernel,
         grid_spec=pltpu.PrefetchScalarGridSpec(
             num_scalar_prefetch=1,
-            grid=(STEPS,),
+            grid=(STEPS + 4,),
             in_specs=[
                 whole(NB, 1, BLK),
                 whole(CODES, LAT),
                 whole(HID, LAT),
                 whole(HID, LAT),
-                pl.BlockSpec((ROWS, TILE), lambda i, s: (0, i)),
-                pl.BlockSpec((HID, TILE), lambda i, s: (0, i)),
-                pl.BlockSpec((TILE, HID), lambda i, s: (i, 0)),
+                pl.BlockSpec((ROWS, TILE), columns),
+                pl.BlockSpec((HID, TILE), columns),
+                pl.BlockSpec((TILE, HID), lambda i, s: (jnp.minimum(i, STEPS - 1), 0)),
             ],
             out_specs=[
-                pl.BlockSpec((HID // 2, TILE), lambda i, s: (0, i)),
-                pl.BlockSpec((HID // 2, TILE), lambda i, s: (0, i)),
+                pl.BlockSpec((HID // 2, TILE), columns),
+                pl.BlockSpec((HID // 2, TILE), columns),
                 whole(ROWS, HID),
                 whole(ROWS, LAT),
-                whole(128, 8, LAT),
+                whole(64, 8, LAT),
+                pl.BlockSpec((16, DROWS, LAT), lambda i, s: (jnp.maximum(i - STEPS, 0), 0, 0)),
             ],
             scratch_shapes=[
                 pltpu.VMEM((ROWS, LAT), BF),
@@ -265,6 +298,8 @@
                 pltpu.VMEM((ROWS, HID), F32),
                 pltpu.VMEM((ROWS, HID), F32),
                 pltpu.VMEM((HID, HID), BF),
+                pltpu.VMEM((ROWS, FEAT), BF),
+                pltpu.VMEM((128, 8, LAT), BF),
             ],
         ),
         out_shape=[
@@ -272,7 +307,8 @@
             jax.ShapeDtypeStruct((HID // 2, FEAT), BF),
             jax.ShapeDtypeStruct((ROWS, HID), BF),
             jax.ShapeDtypeStruct((ROWS, LAT), F32),
-            jax.ShapeDtypeStruct((128, 8, LAT), BF),
+            jax.ShapeDtypeStruct((64, 8, LAT), BF),
+            jax.ShapeDtypeStruct((64, DROWS, LAT), BF),
         ],
         compiler_params=pltpu.CompilerParams(vmem_limit_bytes=60 << 20),
         cost_estimate=pl.CostEstimate(flops=20 * 10**9, bytes_accessed=24 << 20, transcendentals=0),
@@ -304,17 +340,17 @@
         in_specs=[
             pl.BlockSpec((ROWS, FEAT // 4), lambda i: (0, i)),
             whole(ROWS, HID),
-            whole(128, 8, LAT),
+            whole(64, 8, LAT),
         ],
-        out_specs=[whole(64, DROWS, LAT)] * 2,
-        out_shape=[jax.ShapeDtypeStruct((64, DROWS, LAT), BF)] * 2,
+        out_specs=whole(64, DROWS, LAT),
+        out_shape=jax.ShapeDtypeStruct((64, DROWS, LAT), BF),
         compiler_params=pltpu.CompilerParams(vmem_limit_bytes=48 << 20),
-        cost_estimate=pl.CostEstimate(flops=44 * 10**8, bytes_accessed=13 << 20, transcendentals=0),
+        cost_estimate=pl.CostEstimate(flops=22 * 10**8, bytes_accessed=11 << 20, transcendentals=0),
         name="encoder_grads",
     )(x, bh, small)
 
 
-def join(e_own, e_arrived, d_own, d_arrived):
+def join(e_own, e_arrived, d_own, d_far):
     return pl.pallas_call(
         join_kernel,
         out_shape=[jax.ShapeDtypeStruct((4, JROWS, LAT), F32)] + [jax.ShapeDtypeStruct((4, JROWS, LAT), BF)] * 3,
@@ -322,7 +358,7 @@
         compiler_params=pltpu.CompilerParams(vmem_limit_bytes=16 << 20),
         cost_estimate=pl.CostEstimate(flops=10**7, bytes_accessed=6 << 20, transcendentals=0),
         name="sum_first_exchange",
-    )(e_own, *e_arrived, d_own, *d_arrived)
+    )(e_own, *e_arrived, d_own, d_far)
 
 
 def last(own, arrived):
@@ -375,6 +411,10 @@
     return moves(change)
 
 
+def flip_z(phase):
+    return moves(lambda x, y, c, z: (x, y, c, z ^ (1 if (phase == 0) == (c == 0) else 3)))
+
+
 def turn(by):
     return moves(lambda x, y, c, z: (x, y, c, (z + by) % 4))
 
@@ -402,29 +442,34 @@
     expand_weight,
     decoder_weight,
 ):
-    x = frames.reshape(ROWS, FEAT)
-    send, keep, bh, lat, small = main(
+    x = frames.reshape(NB * BLK, FEAT)
+    send, keep, bh, lat, small, e_send = main(
         clip_lengths.reshape(4), frame_codes, codebook, expand_weight, latent_weight, x, decoder_weight, encoder_weight
     )
     d_swap = swap_cores(send)
-    e_send, e_keep = outer(x, bh, small)
     e_swap = swap_cores(e_send)
-
-    d_own, d_shares = first_shares(keep, d_swap, 64)
-    d_arrived = [lax.ppermute(share, BOTH, flip(0, first)) for share, first in zip(d_shares, (3, 2, 1))]
+    e_keep = outer(x, bh, small)
+
+    share = (keep[128:].astype(F32) + d_swap[128:].astype(F32)).astype(BF)
+    d_near = lax.ppermute(share, BOTH, flip_z(0))
+    d_own = keep[:128].astype(F32) + d_swap[:128].astype(F32)
     e_own, e_shares = first_shares(e_keep, e_swap, 16)
     e_arrived = [lax.ppermute(share, BOTH, flip(0, first)) for share, first in zip(e_shares, (3, 2, 1))]
     packed = pack(block_dest.reshape(2 * NB), lat, e_shares[0])
     got = lax.all_to_all(packed, "dp", 0, 0, tiled=True)
 
-    own, *shares = join(e_own, e_arrived, d_own, d_arrived)
-    shares, got = lax.optimization_barrier((shares, got))
+    d_far = lax.ppermute((d_own[64:] + d_near[64:].astype(F32)).astype(BF), BOTH, flip_z(1))
+    d_own = d_own[:64] + d_near[:64].astype(F32)
+    own, *shares = join(e_own, e_arrived, d_own, d_far)
     arrived = [lax.ppermute(shares[by - 1], BOTH, flip(1, by)) for by in (3, 2, 1)]
+    arrived, got = lax.optimization_barrier((arrived, got))
     latents = arrive(got)
     for piece in arrived:
         own = own + piece.astype(F32)
-    arrived = [lax.ppermute(own[by : by + 1].astype(BF), BOTH, turn(by)) for by in (2, 3, 1)]
-    grad_encoder, grad_latent, grad_expand, grad_decoder = last(own[:1], arrived)
+    shares = own.astype(BF)
+    e_arrived = [lax.ppermute(shares[by : by + 1, :DROWS], BOTH, turn(by)) for by in (2, 3, 1)]
+    d_arrived = [lax.ppermute(shares[by : by + 1, DROWS:], BOTH, flip(0, by)) for by in (3, 2, 1)]
+    grad_encoder, grad_latent, grad_expand, grad_decoder = last(own[:1], e_arrived + d_arrived)
     return latents[:, None], grad_encoder, grad_latent, grad_expand, grad_decoder
 
 

time: 106 us -> 97.3 us (0.918)
  waiting for transfers between devices: 23.8 us -> 14.5 us
  local copies, waits for them, and re-layouts: 6.92 us -> 1.52 us
  Pallas kernels: 42.2 us -> 44.2 us
  starting transfers between devices: 28.8 us -> 30.5 us
  other arithmetic: 3.41 us -> 4.97 us
    ppermute x6 -> x3, waiting for transfers between devices: 12.8 us -> 0.01 us  [per_device(): lax.ppermute(share, BOTH, flip(0, first))]
    ppermute x3 -> x8, starting transfers between devices: 5.99 us -> 13.2 us  [the longest x1 4.12 us: per_device(): lax.ppermute((d_own[64:] + d_near[64:].astype(F32)).astype(BF), BOTH, fli...]
    ppermute x6 -> x3, starting transfers between devices: 9.3 us -> 3.49 us  [per_device(): lax.ppermute(share, BOTH, flip(0, first))]
    unnamed x19 -> x9, local copies, waits for them, and re-layouts: 6.81 us -> 1.41 us
    pallas_call x1, Pallas kernels: 28.4 us -> 32.1 us  [main(): pl.pallas_call(main_kernel, grid_spec=pltpu.PrefetchScalarGridSpec(num_sc...]
    convert_element_type x0 -> x3, other arithmetic: none -> 3.42 us  [the longest x1 2.31 us: per_device(): share = (keep[128:].astype(F32) + d_swap[128:].astype(F32)).astype(BF)]
    ppermute x2, waiting for transfers between devices: 0.6 us -> 3.86 us  [swap_cores(): return lax.ppermute(array, BOTH, moves(lambda x, y, c, z: (x, y, 1 - c, z)))]
    pallas_call x1, Pallas kernels: 7.47 us -> 5.58 us  [outer(): pl.pallas_call(outer_kernel, grid=(4,), in_specs=[pl.BlockSpec((ROWS, FEA...]
  transfers between devices with their start and end apart: 15 -> 17, of which waited for: 9 -> 7; matrix products, arithmetic and copies ran while one was open for 3% -> 5% of each run, Pallas kernels for 12% -> 12%
where the time goes in v3:
time: 97.3 us; the launch traced here: 96.5 us
  Pallas kernels  44.2 us (45%)
  starting transfers between devices  30.5 us (31%)
  waiting for transfers between devices  14.5 us (15%)
  other arithmetic  4.97 us (5%)
  local copies, waits for them, and re-layouts  1.52 us (2%)
    pallas_call x1, Pallas kernels, main(): pl.pallas_call(main_kernel, grid_spec=pltpu.PrefetchScalarGridSpec(num_sc...  32.1 us
    all_to_all x1, starting transfers between devices, per_device(): got = lax.all_to_all(packed, 'dp', 0, 0, tiled=True)  7.33 us
    ppermute x3, waiting for transfers between devices, per_device(): lax.ppermute(shares[by - 1], BOTH, flip(1, by))  6.3 us
    ppermute x3, starting transfers between devices, per_device(): lax.ppermute(shares[by - 1], BOTH, flip(1, by))  5.91 us
    pallas_call x1, Pallas kernels, outer(): pl.pallas_call(outer_kernel, grid=(4,), in_specs=[pl.BlockSpec((ROWS, FEA...  5.58 us
    ppermute x1, starting transfers between devices, per_device(): lax.ppermute((d_own[64:] + d_near[64:].astype(F32)).astype(BF), BOTH, fli...  4.12 us
    ppermute x2, waiting for transfers between devices, swap_cores(): return lax.ppermute(array, BOTH, moves(lambda x, y, c, z: (x, y, 1 - c, z)))  3.86 us
    ppermute x3, starting transfers between devices, per_device(): lax.ppermute(shares[by:by + 1, DROWS:], BOTH, flip(0, by))  3.57 us
  transfers between devices with their start and end apart: 17, of which 7 were waited for; matrix products, arithmetic and copies ran while one was open for 5% of the time, Pallas kernels for 12%

profile of v3, /device:TPU:0, one launch (start us, length us, event | category | flops | bytes accessed | tf_op | source)
XLA Modules:
  0.0 96.5 jit_solution(8582951495166931463)
XLA Ops:
  0.6 1.4 %copy.14.codes = s32[64,1,16]{2,1,0:T(1,128)} copy(s32[64,1,16]{0,2,1:T(8,128)} %param.12) | data formatting | bytes 8192 | tf_op args[3]
  2.0 32.1 %forward_and_hidden_grads.1 = (bf16[256,4096]{1,0:T(8,128)(2,1)}, bf16[256,4096]{1,0:T(8,128)(2,1)}, bf16[960,512]{1,0:T(8,128)(2,1)}, f32[960,128]{1,0:T(8,128)...) custom-call(s32[4]{0:T(128)} %bitcast.8, s32[64,1,16]{2,1,0:T(1,128)} %copy.14.codes, ...), custom_call_target="tpu_custom_call" | custom-call | flops 20000000000 | bytes 25165824 | tf_op jit(solution)/shard_map/forward_and_hidden_grads/pallas_call | solution.py:271
  34.1 0.0 collective-permute-start.4
  34.2 0.5 collective-permute-start
  34.7 3.9 %collective-permute-done.4 = bf16[256,4096]{1,0:T(8,128)(2,1)S(1)} collective-permute-done((bf16[256,4096]{1,0:T(8,128)(2,1)}, bf16[256,4096]{1,0:T(8,128)(2,1)S(1)}, u32[]{:S(2)}, u32[]{:S(2)}) %collective-permute-start.4) | collective-permute-done | bytes 2097184 | tf_op jit(solution)/shard_map/ppermute | solution.py:423
  38.5 2.3 %add_convert_fusion = (bf16[128,4096]{1,0:T(8,128)(2,1)S(1)}, f32[128,4096]{1,0:T(8,128)S(1)}) fusion(bf16[256,4096]{1,0:T(8,128)(2,1)S(1)} %collective-permute-done.4, bf16[256,4096]{1,0:T(8,128)(2,1)} %get-tuple-element.26), kind=kLoop, calls=%fused_computation | loop fusion | flops 3670016 | bytes 7340032 | tf_op jit(solution)/shard_map/convert_element_type | solution.py:453
  40.8 2.1 %collective-permute-start.5 = (bf16[128,4096]{1,0:T(8,128)(2,1)S(1)}, bf16[128,4096]{1,0:T(8,128)(2,1)S(1)}, u32[]{:S(2)}, u32[]{:S(2)}) collective-permute-start(bf16[128,4096]{1,0:T(8,128)(2,1)S(1)} %get-tuple-element.52), channel_id=1, source_target_pairs={{0,1},{1,0},{2,3},{3,2},{4,7},{5,6},{6,5},{7,4},{8,9},{9,8},{10,11... | collective-permute-start | bytes 3145736 | tf_op jit(solution)/shard_map/ppermute | solution.py:454
  42.9 0.0 copy-done
  42.9 5.6 %encoder_grads.1 = bf16[64,136,128]{2,1,0:T(8,128)(2,1)S(1)} custom-call(bf16[1024,4096]{1,0:T(8,128)(2,1)} %bitcast.6, bf16[960,512]{1,0:T(8,128)(2,1)S(1)} %copy-done, bf16[64,8,128]{2,1,0:T(8,128)(2,1)S(1)} %copy-done.2), custom_call_target="tpu_custom_call" | custom-call | flops 2200000000 | bytes 11534336 | tf_op jit(solution)/shard_map/encoder_grads/pallas_call | solution.py:337
  48.5 0.0 collective-permute-done
  48.5 1.6 %add_convert_fusion.1 = (bf16[16,136,128]{2,1,0:T(8,128)(2,1)}, bf16[16,136,128]{2,1,0:T(8,128)(2,1)}, bf16[16,136,128]{2,1,0:T(8,128)(2,1)S(1)}, f32[16,136,128]{2,1,0:T(8,128)S(1)}) fusion(bf16[64,136,128]{2,1,0:T(8,128)(2,1)S(1)} %collective-permute-done, bf16[64,136,128]{2,1,0:T(8,128)(2,1)S(1)} %encoder_grads.1), kind=kLoop, calls=%fused_computation.2 | loop fusion | flops 4177920 | bytes 7241728 | tf_op jit(solution)/shard_map/convert_element_type | solution.py:431
  50.1 2.5 %collective-permute-start.1 = (bf16[16,136,128]{2,1,0:T(8,128)(2,1)S(1)}, bf16[16,136,128]{2,1,0:T(8,128)(2,1)}, u32[]{:S(2)}, u32[]{:S(2)}) collective-permute-start(bf16[16,136,128]{2,1,0:T(8,128)(2,1)S(1)} %get-tuple-element.50._), channel_id=1, source_target_pairs={{0,40},{1,41},{2,42},{3,43},{4,124},{5,125},{6,126},{7,127},{8,32}... | collective-permute-start | bytes 1671176 | tf_op jit(solution)/shard_map/ppermute | solution.py:457
  52.6 0.5 collective-permute-start.2
  53.1 0.4 collective-permute-start.3
  53.6 2.2 %collective-permute-done.5 = bf16[128,4096]{1,0:T(8,128)(2,1)S(1)} collective-permute-done((bf16[128,4096]{1,0:T(8,128)(2,1)S(1)}, bf16[128,4096]{1,0:T(8,128)(2,1)S(1)}, u32[]{:S(2)}, u32[]{:S(2)}) %collective-permute-start.5) | collective-permute-done | bytes 1048608 | tf_op jit(solution)/shard_map/ppermute | solution.py:454
  55.7 1.0 %fusion = (bf16[64,4096]{1,0:T(8,128)(2,1)}, f32[64,4096]{1,0:T(8,128)S(1)}) fusion(f32[128,4096]{1,0:T(8,128)S(1)} %get-tuple-element.53, bf16[128,4096]{1,0:T(8,128)(2,1)S(1)} %collective-permute-done.5), kind=kLoop, calls=%fused_computation.7 | loop fusion | flops 1310720 | bytes 4718592 | tf_op jit(solution)/shard_map/convert_element_type | solution.py:461
  56.7 4.1 %collective-permute-start.6 = (bf16[64,4096]{1,0:T(8,128)(2,1)}, bf16[64,4096]{1,0:T(8,128)(2,1)}, u32[]{:S(2)}, u32[]{:S(2)}) collective-permute-start(bf16[64,4096]{1,0:T(8,128)(2,1)} %get-tuple-element.54), channel_id=1, source_target_pairs={{0,3},{1,2},{2,1},{3,0},{4,5},{5,4},{6,7},{7,6},{8,11},{9,10},{10,... | collective-permute-start | bytes 1572872 | tf_op jit(solution)/shard_map/ppermute | solution.py:461
  60.8 0.0 copy-done.3
  60.8 0.1 reshape.21.dest
  60.9 2.2 %pack_latents.1 = bf16[32,40,128]{2,1,0:T(8,128)(2,1)} custom-call(s32[128]{0:T(128)S(1)} %reshape.21.dest, f32[960,128]{1,0:T(8,128)S(1)} %copy-done.1, bf16[16,136,128]{2,1,0:T(8,128)(2,1)S(1)} %get-tuple-element.50._), custom_call_target="tpu_custom_call" | custom-call | flops 1000000 | bytes 1048576 | tf_op jit(solution)/shard_map/pack_latents/pallas_call | solution.py:320
  63.1 7.3 %all-to-all-start = ((bf16[32,40,128]{2,1,0:T(8,128)(2,1)}), bf16[32,40,128]{2,1,0:T(8,128)(2,1)S(1)}, u32[]{:S(2)}, u32[]{:S(2)}) async-start(bf16[32,40,128]{2,1,0:T(8,128)(2,1)} %pack_latents.1), calls=%async_computation | async-start | bytes 655360 | tf_op jit(solution)/shard_map/all_to_all | solution.py:459
  70.4 0.0 collective-permute-done.1.e3
  70.4 0.0 collective-permute-done.2.e2
  70.5 0.0 collective-permute-done.3.e1
  70.5 0.0 collective-permute-done.6.d_far
  70.5 2.5 %sum_first_exchange.1 = (f32[4,264,128]{2,1,0:T(8,128)S(1)}, bf16[4,264,128]{2,1,0:T(8,128)(2,1)S(1)}, bf16[4,264,128]{2,1,0:T(8,128)(2,1)}, bf16[4,264,128]{2,1,0:T(8,128)(2,1)}) custom-call(f32[16,136,128]{2,1,0:T(8,128)S(1)} %get-tuple-element.51.own_e, bf16[16,136,128]{2,1,0:T(8,128)(2,1)} %collective-permute-done.1.e3, ...), custom_call_target="tpu_custom_call" | custom-call | flops 10000000 | bytes 6291456 | tf_op jit(solution)/shard_map/sum_first_exchange/pallas_call | solution.py:354
  72.9 5.2 %collective-permute-start.7 = (bf16[4,264,128]{2,1,0:T(8,128)(2,1)}, bf16[4,264,128]{2,1,0:T(8,128)(2,1)S(1)}, u32[]{:S(2)}, u32[]{:S(2)}) collective-permute-start(bf16[4,264,128]{2,1,0:T(8,128)(2,1)} %get-tuple-element.28), channel_id=1, source_target_pairs={{0,120},{1,121},{2,122},{3,123},{4,44},{5,45},{6,46},{7,47},{8,112... | collective-permute-start | bytes 811016 | tf_op jit(solution)/shard_map/ppermute | solution.py:464
  78.1 0.5 collective-permute-start.8
  78.6 0.2 collective-permute-start.9
  78.8 1.1 %all-to-all-done.got = bf16[32,40,128]{2,1,0:T(8,128)(2,1)S(1)} async-done(((bf16[32,40,128]{2,1,0:T(8,128)(2,1)}), bf16[32,40,128]{2,1,0:T(8,128)(2,1)S(1)}, u32[]{:S(2)}, u32[]{:S(2)}) %all-to-all-start) | async-done | bytes 327712 | tf_op jit(solution)/shard_map/all_to_all | solution.py:459
  80.0 3.3 %collective-permute-done.7 = bf16[4,264,128]{2,1,0:T(8,128)(2,1)S(1)} collective-permute-done((bf16[4,264,128]{2,1,0:T(8,128)(2,1)}, bf16[4,264,128]{2,1,0:T(8,128)(2,1)S(1)}, u32[]{:S(2)}, u32[]{:S(2)}) %collective-permute-start.7) | collective-permute-done | bytes 270368 | tf_op jit(solution)/shard_map/ppermute | solution.py:464
  83.3 2.9 %collective-permute-done.8 = bf16[4,264,128]{2,1,0:T(8,128)(2,1)S(1)} collective-permute-done((bf16[4,264,128]{2,1,0:T(8,128)(2,1)}, bf16[4,264,128]{2,1,0:T(8,128)(2,1)S(1)}, u32[]{:S(2)}, u32[]{:S(2)}) %collective-permute-start.8) | collective-permute-done | bytes 270368 | tf_op jit(solution)/shard_map/ppermute | solution.py:464
  86.2 0.1 collective-permute-done.9
  86.3 0.1 fusion.1
  86.4 0.2 collective-permute-start.13
  86.7 1.5 %collective-permute-start.10 = (bf16[1,136,128]{2,1,0:T(8,128)(2,1)S(1)}, bf16[1,136,128]{2,1,0:T(8,128)(2,1)S(1)}, u32[]{:S(2)}, u32[]{:S(2)}) collective-permute-start(bf16[1,136,128]{2,1,0:T(8,128)(2,1)S(1)} %get-tuple-element.61), channel_id=1, source_target_pairs={{0,2},{1,3},{2,0},{3,1},{4,6},{5,7},{6,4},{7,5},{8,10},{9,11},{10,... | collective-permute-start | bytes 104456 | tf_op jit(solution)/shard_map/ppermute | solution.py:470
  88.2 1.2 %collective-permute-start.11 = (bf16[1,136,128]{2,1,0:T(8,128)(2,1)S(1)}, bf16[1,136,128]{2,1,0:T(8,128)(2,1)S(1)}, u32[]{:S(2)}, u32[]{:S(2)}) collective-permute-start(bf16[1,136,128]{2,1,0:T(8,128)(2,1)S(1)} %get-tuple-element.60), channel_id=1, source_target_pairs={{0,3},{1,0},{2,1},{3,2},{4,7},{5,4},{6,5},{7,6},{8,11},{9,8},{10,9... | collective-permute-start | bytes 104456 | tf_op jit(solution)/shard_map/ppermute | solution.py:470
  89.4 0.8 collective-permute-start.12
  90.2 1.7 %collective-permute-start.14 = (bf16[1,128,128]{2,1,0:T(8,128)(2,1)S(1)}, bf16[1,128,128]{2,1,0:T(8,128)(2,1)S(1)}, u32[]{:S(2)}, u32[]{:S(2)}) collective-permute-start(bf16[1,128,128]{2,1,0:T(8,128)(2,1)S(1)} %get-tuple-element.57), channel_id=1, source_target_pairs={{0,32},{1,33},{2,34},{3,35},{4,100},{5,101},{6,102},{7,103},{8,40}... | collective-permute-start | bytes 98312 | tf_op jit(solution)/shard_map/ppermute | solution.py:471
  91.8 0.0 collective-permute-done.13.d3
  91.9 1.7 %collective-permute-start.15 = (bf16[1,128,128]{2,1,0:T(8,128)(2,1)S(1)}, bf16[1,128,128]{2,1,0:T(8,128)(2,1)S(1)}, u32[]{:S(2)}, u32[]{:S(2)}) collective-permute-start(bf16[1,128,128]{2,1,0:T(8,128)(2,1)S(1)} %get-tuple-element.56), channel_id=1, source_target_pairs={{0,8},{1,9},{2,10},{3,11},{4,28},{5,29},{6,30},{7,31},{8,0},{9,1},... | collective-permute-start | bytes 98312 | tf_op jit(solution)/shard_map/ppermute | solution.py:471
  93.5 1.2 %place_latents.1 = f32[32,16,128]{2,1,0:T(8,128)} custom-call(bf16[32,40,128]{2,1,0:T(8,128)(2,1)S(1)} %all-to-all-done.got), custom_call_target="tpu_custom_call" | custom-call | flops 1000000 | bytes 1048576 | tf_op jit(solution)/shard_map/place_latents/pallas_call | solution.py:380
  94.7 0.0 collective-permute-done.14.d2
  94.7 1.0 %collective-permute-done.15.d1 = bf16[1,128,128]{2,1,0:T(8,128)(2,1)S(1)} collective-permute-done((bf16[1,128,128]{2,1,0:T(8,128)(2,1)S(1)}, bf16[1,128,128]{2,1,0:T(8,128)(2,1)S(1)}, u32[]{:S(2)}, u32[]{:S(2)}) %collective-permute-start.15) | collective-permute-done | bytes 32800 | tf_op jit(solution)/shard_map/ppermute | solution.py:471
  95.8 0.0 collective-permute-done.10.e3
  95.8 0.0 collective-permute-done.11.e2
  95.8 0.0 collective-permute-done.12.e1
  95.8 0.7 sum_last_exchange.1
  (9 shorter events, 0.0 us)
Async XLA Ops:
  34.1 4.4 %collective-permute-start.4 = (bf16[256,4096]{1,0:T(8,128)(2,1)}, bf16[256,4096]{1,0:T(8,128)(2,1)S(1)}, u32[]{:S(2)}, u32[]{:S(2)}) collective-permute-start(bf16[256,4096]{1,0:T(8,128)(2,1)} %get-tuple-element.27), channel_id=1, source_target_pairs={{0,4},{1,5},{2,6},{3,7},{4,0},{5,1},{6,2},{7,3},{8,12},{9,13},{10,... | collective-permute-start | bytes 6291464 | tf_op jit(solution)/shard_map/ppermute | solution.py:423
  34.2 14.4 %collective-permute-start = (bf16[64,136,128]{2,1,0:T(8,128)(2,1)}, bf16[64,136,128]{2,1,0:T(8,128)(2,1)S(1)}, u32[]{:S(2)}, u32[]{:S(2)}) collective-permute-start(bf16[64,136,128]{2,1,0:T(8,128)(2,1)} %get-tuple-element.25), channel_id=1, source_target_pairs={{0,4},{1,5},{2,6},{3,7},{4,0},{5,1},{6,2},{7,3},{8,12},{9,13},{10,... | collective-permute-start | bytes 6684680 | tf_op jit(solution)/shard_map/ppermute | solution.py:423
  38.5 4.4 %copy-start = (bf16[960,512]{1,0:T(8,128)(2,1)S(1)}, bf16[960,512]{1,0:T(8,128)(2,1)}, u32[]{:S(2)}) copy-start(bf16[960,512]{1,0:T(8,128)(2,1)} %get-tuple-element.23.bh) | copy-start | bytes 2949124
  38.5 4.4 %copy-start.2 = (bf16[64,8,128]{2,1,0:T(8,128)(2,1)S(1)}, bf16[64,8,128]{2,1,0:T(8,128)(2,1)}, u32[]{:S(2)}) copy-start(bf16[64,8,128]{2,1,0:T(8,128)(2,1)} %get-tuple-element.24.small) | copy-start | bytes 393220
  40.8 14.9 %collective-permute-start.5 = (bf16[128,4096]{1,0:T(8,128)(2,1)S(1)}, bf16[128,4096]{1,0:T(8,128)(2,1)S(1)}, u32[]{:S(2)}, u32[]{:S(2)}) collective-permute-start(bf16[128,4096]{1,0:T(8,128)(2,1)S(1)} %get-tuple-element.52), channel_id=1, source_target_pairs={{0,1},{1,0},{2,3},{3,2},{4,7},{5,6},{6,5},{7,4},{8,9},{9,8},{10,11... | collective-permute-start | bytes 3145736 | tf_op jit(solution)/shard_map/ppermute | solution.py:454
  50.1 20.4 %collective-permute-start.1 = (bf16[16,136,128]{2,1,0:T(8,128)(2,1)S(1)}, bf16[16,136,128]{2,1,0:T(8,128)(2,1)}, u32[]{:S(2)}, u32[]{:S(2)}) collective-permute-start(bf16[16,136,128]{2,1,0:T(8,128)(2,1)S(1)} %get-tuple-element.50._), channel_id=1, source_target_pairs={{0,40},{1,41},{2,42},{3,43},{4,124},{5,125},{6,126},{7,127},{8,32}... | collective-permute-start | bytes 1671176 | tf_op jit(solution)/shard_map/ppermute | solution.py:457
  52.6 17.9 %collective-permute-start.2 = (bf16[16,136,128]{2,1,0:T(8,128)(2,1)}, bf16[16,136,128]{2,1,0:T(8,128)(2,1)}, u32[]{:S(2)}, u32[]{:S(2)}) collective-permute-start(bf16[16,136,128]{2,1,0:T(8,128)(2,1)} %get-tuple-element.49), channel_id=1, source_target_pairs={{0,32},{1,33},{2,34},{3,35},{4,100},{5,101},{6,102},{7,103},{8,40}... | collective-permute-start | bytes 1671176 | tf_op jit(solution)/shard_map/ppermute | solution.py:457
  53.1 17.3 %collective-permute-start.3 = (bf16[16,136,128]{2,1,0:T(8,128)(2,1)}, bf16[16,136,128]{2,1,0:T(8,128)(2,1)}, u32[]{:S(2)}, u32[]{:S(2)}) collective-permute-start(bf16[16,136,128]{2,1,0:T(8,128)(2,1)} %get-tuple-element.48), channel_id=1, source_target_pairs={{0,8},{1,9},{2,10},{3,11},{4,28},{5,29},{6,30},{7,31},{8,0},{9,1},... | collective-permute-start | bytes 1671176 | tf_op jit(solution)/shard_map/ppermute | solution.py:457
  55.7 5.1 %copy-start.3 = (s32[1,1,2,64]{3,2,1,0:T(2,128)S(1)}, s32[1,1,2,64]{3,2,1,0:T(2,128)}, u32[]{:S(2)}) copy-start(s32[1,1,2,64]{3,2,1,0:T(2,128)} %param.11) | copy-start | bytes 1540
  55.7 5.2 %copy-start.1 = (f32[960,128]{1,0:T(8,128)S(1)}, f32[960,128]{1,0:T(8,128)}, u32[]{:S(2)}) copy-start(f32[960,128]{1,0:T(8,128)} %get-tuple-element.31.lat) | copy-start | bytes 1474564
  56.7 13.8 %collective-permute-start.6 = (bf16[64,4096]{1,0:T(8,128)(2,1)}, bf16[64,4096]{1,0:T(8,128)(2,1)}, u32[]{:S(2)}, u32[]{:S(2)}) collective-permute-start(bf16[64,4096]{1,0:T(8,128)(2,1)} %get-tuple-element.54), channel_id=1, source_target_pairs={{0,3},{1,2},{2,1},{3,0},{4,5},{5,4},{6,7},{7,6},{8,11},{9,10},{10,... | collective-permute-start | bytes 1572872 | tf_op jit(solution)/shard_map/ppermute | solution.py:461
  63.1 16.9 %all-to-all-start = ((bf16[32,40,128]{2,1,0:T(8,128)(2,1)}), bf16[32,40,128]{2,1,0:T(8,128)(2,1)S(1)}, u32[]{:S(2)}, u32[]{:S(2)}) async-start(bf16[32,40,128]{2,1,0:T(8,128)(2,1)} %pack_latents.1), calls=%async_computation | async-start | bytes 655360 | tf_op jit(solution)/shard_map/all_to_all | solution.py:459
  72.9 10.3 %collective-permute-start.7 = (bf16[4,264,128]{2,1,0:T(8,128)(2,1)}, bf16[4,264,128]{2,1,0:T(8,128)(2,1)S(1)}, u32[]{:S(2)}, u32[]{:S(2)}) collective-permute-start(bf16[4,264,128]{2,1,0:T(8,128)(2,1)} %get-tuple-element.28), channel_id=1, source_target_pairs={{0,120},{1,121},{2,122},{3,123},{4,44},{5,45},{6,46},{7,47},{8,112... | collective-permute-start | bytes 811016 | tf_op jit(solution)/shard_map/ppermute | solution.py:464
  78.1 8.0 %collective-permute-start.8 = (bf16[4,264,128]{2,1,0:T(8,128)(2,1)}, bf16[4,264,128]{2,1,0:T(8,128)(2,1)S(1)}, u32[]{:S(2)}, u32[]{:S(2)}) collective-permute-start(bf16[4,264,128]{2,1,0:T(8,128)(2,1)} %get-tuple-element.29), channel_id=1, source_target_pairs={{0,96},{1,97},{2,98},{3,99},{4,36},{5,37},{6,38},{7,39},{8,104},{9... | collective-permute-start | bytes 811016 | tf_op jit(solution)/shard_map/ppermute | solution.py:464
  78.6 7.7 %collective-permute-start.9 = (bf16[4,264,128]{2,1,0:T(8,128)(2,1)S(1)}, bf16[4,264,128]{2,1,0:T(8,128)(2,1)S(1)}, u32[]{:S(2)}, u32[]{:S(2)}) collective-permute-start(bf16[4,264,128]{2,1,0:T(8,128)(2,1)S(1)} %get-tuple-element.30), channel_id=1, source_target_pairs={{0,24},{1,25},{2,26},{3,27},{4,12},{5,13},{6,14},{7,15},{8,16},{9,... | collective-permute-start | bytes 811016 | tf_op jit(solution)/shard_map/ppermute | solution.py:464
  86.4 5.4 %collective-permute-start.13 = (bf16[1,128,128]{2,1,0:T(8,128)(2,1)S(1)}, bf16[1,128,128]{2,1,0:T(8,128)(2,1)S(1)}, u32[]{:S(2)}, u32[]{:S(2)}) collective-permute-start(bf16[1,128,128]{2,1,0:T(8,128)(2,1)S(1)} %get-tuple-element.58), channel_id=1, source_target_pairs={{0,40},{1,41},{2,42},{3,43},{4,124},{5,125},{6,126},{7,127},{8,32}... | collective-permute-start | bytes 98312 | tf_op jit(solution)/shard_map/ppermute | solution.py:471
  86.7 9.1 %collective-permute-start.10 = (bf16[1,136,128]{2,1,0:T(8,128)(2,1)S(1)}, bf16[1,136,128]{2,1,0:T(8,128)(2,1)S(1)}, u32[]{:S(2)}, u32[]{:S(2)}) collective-permute-start(bf16[1,136,128]{2,1,0:T(8,128)(2,1)S(1)} %get-tuple-element.61), channel_id=1, source_target_pairs={{0,2},{1,3},{2,0},{3,1},{4,6},{5,7},{6,4},{7,5},{8,10},{9,11},{10,... | collective-permute-start | bytes 104456 | tf_op jit(solution)/shard_map/ppermute | solution.py:470
  88.2 7.6 %collective-permute-start.11 = (bf16[1,136,128]{2,1,0:T(8,128)(2,1)S(1)}, bf16[1,136,128]{2,1,0:T(8,128)(2,1)S(1)}, u32[]{:S(2)}, u32[]{:S(2)}) collective-permute-start(bf16[1,136,128]{2,1,0:T(8,128)(2,1)S(1)} %get-tuple-element.60), channel_id=1, source_target_pairs={{0,3},{1,0},{2,1},{3,2},{4,7},{5,4},{6,5},{7,6},{8,11},{9,8},{10,9... | collective-permute-start | bytes 104456 | tf_op jit(solution)/shard_map/ppermute | solution.py:470
  89.4 6.4 %collective-permute-start.12 = (bf16[1,136,128]{2,1,0:T(8,128)(2,1)S(1)}, bf16[1,136,128]{2,1,0:T(8,128)(2,1)S(1)}, u32[]{:S(2)}, u32[]{:S(2)}) collective-permute-start(bf16[1,136,128]{2,1,0:T(8,128)(2,1)S(1)} %get-tuple-element.59), channel_id=1, source_target_pairs={{0,1},{1,2},{2,3},{3,0},{4,5},{5,6},{6,7},{7,4},{8,9},{9,10},{10,1... | collective-permute-start | bytes 104456 | tf_op jit(solution)/shard_map/ppermute | solution.py:470
  90.2 4.5 %collective-permute-start.14 = (bf16[1,128,128]{2,1,0:T(8,128)(2,1)S(1)}, bf16[1,128,128]{2,1,0:T(8,128)(2,1)S(1)}, u32[]{:S(2)}, u32[]{:S(2)}) collective-permute-start(bf16[1,128,128]{2,1,0:T(8,128)(2,1)S(1)} %get-tuple-element.57), channel_id=1, source_target_pairs={{0,32},{1,33},{2,34},{3,35},{4,100},{5,101},{6,102},{7,103},{8,40}... | collective-permute-start | bytes 98312 | tf_op jit(solution)/shard_map/ppermute | solution.py:471
  91.9 3.9 %collective-permute-start.15 = (bf16[1,128,128]{2,1,0:T(8,128)(2,1)S(1)}, bf16[1,128,128]{2,1,0:T(8,128)(2,1)S(1)}, u32[]{:S(2)}, u32[]{:S(2)}) collective-permute-start(bf16[1,128,128]{2,1,0:T(8,128)(2,1)S(1)} %get-tuple-element.56), channel_id=1, source_target_pairs={{0,8},{1,9},{2,10},{3,11},{4,28},{5,29},{6,30},{7,31},{8,0},{9,1},... | collective-permute-start | bytes 98312 | tf_op jit(solution)/shard_map/ppermute | solution.py:471

commit v4 on v3

--- a/solution.py
+++ b/solution.py
@@ -20,7 +20,7 @@
 META = 2 * BLK + 8
 DROWS = 136
 JROWS = DROWS + 128
-TILE = 512
+TILE = 1024
 STEPS = FEAT // TILE
 BF = jnp.bfloat16
 F32 = jnp.float32

time: 97.3 us -> 97.2 us (level)
  no operation moved by 1% of the time
where the time goes in v4:
time: 97.2 us; the launch traced here: 96.3 us
  Pallas kernels  44 us (45%)
  starting transfers between devices  30.6 us (31%)
  waiting for transfers between devices  14.5 us (15%)
  other arithmetic  4.97 us (5%)
  local copies, waits for them, and re-layouts  1.52 us (2%)
    pallas_call x1, Pallas kernels, main(): pl.pallas_call(main_kernel, grid_spec=pltpu.PrefetchScalarGridSpec(num_sc...  31.9 us
    all_to_all x1, starting transfers between devices, per_device(): got = lax.all_to_all(packed, 'dp', 0, 0, tiled=True)  7.34 us
    ppermute x3, waiting for transfers between devices, per_device(): lax.ppermute(shares[by - 1], BOTH, flip(1, by))  6.3 us
    ppermute x3, starting transfers between devices, per_device(): lax.ppermute(shares[by - 1], BOTH, flip(1, by))  5.91 us
    pallas_call x1, Pallas kernels, outer(): pl.pallas_call(outer_kernel, grid=(4,), in_specs=[pl.BlockSpec((ROWS, FEA...  5.59 us
    ppermute x1, starting transfers between devices, per_device(): lax.ppermute((d_own[64:] + d_near[64:].astype(F32)).astype(BF), BOTH, fli...  4.14 us
    ppermute x2, waiting for transfers between devices, swap_cores(): return lax.ppermute(array, BOTH, moves(lambda x, y, c, z: (x, y, 1 - c, z)))  3.86 us
    ppermute x3, starting transfers between devices, per_device(): lax.ppermute(shares[by:by + 1, DROWS:], BOTH, flip(0, by))  3.57 us
  transfers between devices with their start and end apart: 17, of which 7 were waited for; matrix products, arithmetic and copies ran while one was open for 5% of the time, Pallas kernels for 12%

profile of v4, /device:TPU:0, one launch (start us, length us, event | category | flops | bytes accessed | tf_op | source)
XLA Modules:
  0.0 96.3 jit_solution(3814933716471058882)
XLA Ops:
  0.6 1.4 %copy.14.codes = s32[64,1,16]{2,1,0:T(1,128)} copy(s32[64,1,16]{0,2,1:T(8,128)} %param.12) | data formatting | bytes 8192 | tf_op args[3]
  2.0 31.9 %forward_and_hidden_grads.1 = (bf16[256,4096]{1,0:T(8,128)(2,1)}, bf16[256,4096]{1,0:T(8,128)(2,1)}, bf16[960,512]{1,0:T(8,128)(2,1)}, f32[960,128]{1,0:T(8,128)...) custom-call(s32[4]{0:T(128)} %bitcast.8, s32[64,1,16]{2,1,0:T(1,128)} %copy.14.codes, ...), custom_call_target="tpu_custom_call" | custom-call | flops 20000000000 | bytes 25165824 | tf_op jit(solution)/shard_map/forward_and_hidden_grads/pallas_call | solution.py:271
  33.9 0.0 collective-permute-start.4
  33.9 0.5 collective-permute-start
  34.4 3.9 %collective-permute-done.4 = bf16[256,4096]{1,0:T(8,128)(2,1)S(1)} collective-permute-done((bf16[256,4096]{1,0:T(8,128)(2,1)}, bf16[256,4096]{1,0:T(8,128)(2,1)S(1)}, u32[]{:S(2)}, u32[]{:S(2)}) %collective-permute-start.4) | collective-permute-done | bytes 2097184 | tf_op jit(solution)/shard_map/ppermute | solution.py:423
  38.3 2.3 %add_convert_fusion = (bf16[128,4096]{1,0:T(8,128)(2,1)S(1)}, f32[128,4096]{1,0:T(8,128)S(1)}) fusion(bf16[256,4096]{1,0:T(8,128)(2,1)S(1)} %collective-permute-done.4, bf16[256,4096]{1,0:T(8,128)(2,1)} %get-tuple-element.26), kind=kLoop, calls=%fused_computation | loop fusion | flops 3670016 | bytes 7340032 | tf_op jit(solution)/shard_map/convert_element_type | solution.py:453
  40.6 2.1 %collective-permute-start.5 = (bf16[128,4096]{1,0:T(8,128)(2,1)S(1)}, bf16[128,4096]{1,0:T(8,128)(2,1)S(1)}, u32[]{:S(2)}, u32[]{:S(2)}) collective-permute-start(bf16[128,4096]{1,0:T(8,128)(2,1)S(1)} %get-tuple-element.52), channel_id=1, source_target_pairs={{0,1},{1,0},{2,3},{3,2},{4,7},{5,6},{6,5},{7,4},{8,9},{9,8},{10,11... | collective-permute-start | bytes 3145736 | tf_op jit(solution)/shard_map/ppermute | solution.py:454
  42.7 0.0 copy-done
  42.7 0.0 copy-done.2
  42.7 5.6 %encoder_grads.1 = bf16[64,136,128]{2,1,0:T(8,128)(2,1)S(1)} custom-call(bf16[1024,4096]{1,0:T(8,128)(2,1)} %bitcast.6, bf16[960,512]{1,0:T(8,128)(2,1)S(1)} %copy-done, bf16[64,8,128]{2,1,0:T(8,128)(2,1)S(1)} %copy-done.2), custom_call_target="tpu_custom_call" | custom-call | flops 2200000000 | bytes 11534336 | tf_op jit(solution)/shard_map/encoder_grads/pallas_call | solution.py:337
  48.3 0.0 collective-permute-done
  48.3 1.6 %add_convert_fusion.1 = (bf16[16,136,128]{2,1,0:T(8,128)(2,1)}, bf16[16,136,128]{2,1,0:T(8,128)(2,1)}, bf16[16,136,128]{2,1,0:T(8,128)(2,1)S(1)}, f32[16,136,128]{2,1,0:T(8,128)S(1)}) fusion(bf16[64,136,128]{2,1,0:T(8,128)(2,1)S(1)} %collective-permute-done, bf16[64,136,128]{2,1,0:T(8,128)(2,1)S(1)} %encoder_grads.1), kind=kLoop, calls=%fused_computation.2 | loop fusion | flops 4177920 | bytes 7241728 | tf_op jit(solution)/shard_map/convert_element_type | solution.py:431
  49.9 2.5 %collective-permute-start.1 = (bf16[16,136,128]{2,1,0:T(8,128)(2,1)S(1)}, bf16[16,136,128]{2,1,0:T(8,128)(2,1)}, u32[]{:S(2)}, u32[]{:S(2)}) collective-permute-start(bf16[16,136,128]{2,1,0:T(8,128)(2,1)S(1)} %get-tuple-element.50._), channel_id=1, source_target_pairs={{0,40},{1,41},{2,42},{3,43},{4,124},{5,125},{6,126},{7,127},{8,32}... | collective-permute-start | bytes 1671176 | tf_op jit(solution)/shard_map/ppermute | solution.py:457
  52.4 0.5 collective-permute-start.2
  52.9 0.5 collective-permute-start.3
  53.4 2.1 %collective-permute-done.5 = bf16[128,4096]{1,0:T(8,128)(2,1)S(1)} collective-permute-done((bf16[128,4096]{1,0:T(8,128)(2,1)S(1)}, bf16[128,4096]{1,0:T(8,128)(2,1)S(1)}, u32[]{:S(2)}, u32[]{:S(2)}) %collective-permute-start.5) | collective-permute-done | bytes 1048608 | tf_op jit(solution)/shard_map/ppermute | solution.py:454
  55.5 1.0 %fusion = (bf16[64,4096]{1,0:T(8,128)(2,1)}, f32[64,4096]{1,0:T(8,128)S(1)}) fusion(f32[128,4096]{1,0:T(8,128)S(1)} %get-tuple-element.53, bf16[128,4096]{1,0:T(8,128)(2,1)S(1)} %collective-permute-done.5), kind=kLoop, calls=%fused_computation.7 | loop fusion | flops 1310720 | bytes 4718592 | tf_op jit(solution)/shard_map/convert_element_type | solution.py:461
  56.5 4.1 %collective-permute-start.6 = (bf16[64,4096]{1,0:T(8,128)(2,1)}, bf16[64,4096]{1,0:T(8,128)(2,1)}, u32[]{:S(2)}, u32[]{:S(2)}) collective-permute-start(bf16[64,4096]{1,0:T(8,128)(2,1)} %get-tuple-element.54), channel_id=1, source_target_pairs={{0,3},{1,2},{2,1},{3,0},{4,5},{5,4},{6,7},{7,6},{8,11},{9,10},{10,... | collective-permute-start | bytes 1572872 | tf_op jit(solution)/shard_map/ppermute | solution.py:461
  60.6 0.1 reshape.21.dest
  60.7 2.2 %pack_latents.1 = bf16[32,40,128]{2,1,0:T(8,128)(2,1)} custom-call(s32[128]{0:T(128)S(1)} %reshape.21.dest, f32[960,128]{1,0:T(8,128)S(1)} %copy-done.1, bf16[16,136,128]{2,1,0:T(8,128)(2,1)S(1)} %get-tuple-element.50._), custom_call_target="tpu_custom_call" | custom-call | flops 1000000 | bytes 1048576 | tf_op jit(solution)/shard_map/pack_latents/pallas_call | solution.py:320
  62.9 7.3 %all-to-all-start = ((bf16[32,40,128]{2,1,0:T(8,128)(2,1)}), bf16[32,40,128]{2,1,0:T(8,128)(2,1)S(1)}, u32[]{:S(2)}, u32[]{:S(2)}) async-start(bf16[32,40,128]{2,1,0:T(8,128)(2,1)} %pack_latents.1), calls=%async_computation | async-start | bytes 655360 | tf_op jit(solution)/shard_map/all_to_all | solution.py:459
  70.3 0.0 collective-permute-done.1.e3
  70.3 0.0 collective-permute-done.2.e2
  70.3 0.0 collective-permute-done.3.e1
  70.3 0.0 collective-permute-done.6.d_far
  70.3 2.5 %sum_first_exchange.1 = (f32[4,264,128]{2,1,0:T(8,128)S(1)}, bf16[4,264,128]{2,1,0:T(8,128)(2,1)S(1)}, bf16[4,264,128]{2,1,0:T(8,128)(2,1)}, bf16[4,264,128]{2,1,0:T(8,128)(2,1)}) custom-call(f32[16,136,128]{2,1,0:T(8,128)S(1)} %get-tuple-element.51.own_e, bf16[16,136,128]{2,1,0:T(8,128)(2,1)} %collective-permute-done.1.e3, ...), custom_call_target="tpu_custom_call" | custom-call | flops 10000000 | bytes 6291456 | tf_op jit(solution)/shard_map/sum_first_exchange/pallas_call | solution.py:354
  72.8 5.2 %collective-permute-start.7 = (bf16[4,264,128]{2,1,0:T(8,128)(2,1)}, bf16[4,264,128]{2,1,0:T(8,128)(2,1)S(1)}, u32[]{:S(2)}, u32[]{:S(2)}) collective-permute-start(bf16[4,264,128]{2,1,0:T(8,128)(2,1)} %get-tuple-element.28), channel_id=1, source_target_pairs={{0,120},{1,121},{2,122},{3,123},{4,44},{5,45},{6,46},{7,47},{8,112... | collective-permute-start | bytes 811016 | tf_op jit(solution)/shard_map/ppermute | solution.py:464
  78.0 0.5 collective-permute-start.8
  78.4 0.2 collective-permute-start.9
  78.7 1.1 %all-to-all-done.got = bf16[32,40,128]{2,1,0:T(8,128)(2,1)S(1)} async-done(((bf16[32,40,128]{2,1,0:T(8,128)(2,1)}), bf16[32,40,128]{2,1,0:T(8,128)(2,1)S(1)}, u32[]{:S(2)}, u32[]{:S(2)}) %all-to-all-start) | async-done | bytes 327712 | tf_op jit(solution)/shard_map/all_to_all | solution.py:459
  79.8 3.3 %collective-permute-done.7 = bf16[4,264,128]{2,1,0:T(8,128)(2,1)S(1)} collective-permute-done((bf16[4,264,128]{2,1,0:T(8,128)(2,1)}, bf16[4,264,128]{2,1,0:T(8,128)(2,1)S(1)}, u32[]{:S(2)}, u32[]{:S(2)}) %collective-permute-start.7) | collective-permute-done | bytes 270368 | tf_op jit(solution)/shard_map/ppermute | solution.py:464
  83.1 2.9 %collective-permute-done.8 = bf16[4,264,128]{2,1,0:T(8,128)(2,1)S(1)} collective-permute-done((bf16[4,264,128]{2,1,0:T(8,128)(2,1)}, bf16[4,264,128]{2,1,0:T(8,128)(2,1)S(1)}, u32[]{:S(2)}, u32[]{:S(2)}) %collective-permute-start.8) | collective-permute-done | bytes 270368 | tf_op jit(solution)/shard_map/ppermute | solution.py:464
  86.0 0.1 collective-permute-done.9
  86.1 0.1 fusion.1
  86.3 0.2 collective-permute-start.13
  86.5 1.5 %collective-permute-start.10 = (bf16[1,136,128]{2,1,0:T(8,128)(2,1)S(1)}, bf16[1,136,128]{2,1,0:T(8,128)(2,1)S(1)}, u32[]{:S(2)}, u32[]{:S(2)}) collective-permute-start(bf16[1,136,128]{2,1,0:T(8,128)(2,1)S(1)} %get-tuple-element.61), channel_id=1, source_target_pairs={{0,2},{1,3},{2,0},{3,1},{4,6},{5,7},{6,4},{7,5},{8,10},{9,11},{10,... | collective-permute-start | bytes 104456 | tf_op jit(solution)/shard_map/ppermute | solution.py:470
  88.0 1.2 %collective-permute-start.11 = (bf16[1,136,128]{2,1,0:T(8,128)(2,1)S(1)}, bf16[1,136,128]{2,1,0:T(8,128)(2,1)S(1)}, u32[]{:S(2)}, u32[]{:S(2)}) collective-permute-start(bf16[1,136,128]{2,1,0:T(8,128)(2,1)S(1)} %get-tuple-element.60), channel_id=1, source_target_pairs={{0,3},{1,0},{2,1},{3,2},{4,7},{5,4},{6,5},{7,6},{8,11},{9,8},{10,9... | collective-permute-start | bytes 104456 | tf_op jit(solution)/shard_map/ppermute | solution.py:470
  89.2 0.9 collective-permute-start.12
  90.0 1.7 %collective-permute-start.14 = (bf16[1,128,128]{2,1,0:T(8,128)(2,1)S(1)}, bf16[1,128,128]{2,1,0:T(8,128)(2,1)S(1)}, u32[]{:S(2)}, u32[]{:S(2)}) collective-permute-start(bf16[1,128,128]{2,1,0:T(8,128)(2,1)S(1)} %get-tuple-element.57), channel_id=1, source_target_pairs={{0,32},{1,33},{2,34},{3,35},{4,100},{5,101},{6,102},{7,103},{8,40}... | collective-permute-start | bytes 98312 | tf_op jit(solution)/shard_map/ppermute | solution.py:471
  91.7 0.0 collective-permute-done.13.d3
  91.7 1.7 %collective-permute-start.15 = (bf16[1,128,128]{2,1,0:T(8,128)(2,1)S(1)}, bf16[1,128,128]{2,1,0:T(8,128)(2,1)S(1)}, u32[]{:S(2)}, u32[]{:S(2)}) collective-permute-start(bf16[1,128,128]{2,1,0:T(8,128)(2,1)S(1)} %get-tuple-element.56), channel_id=1, source_target_pairs={{0,8},{1,9},{2,10},{3,11},{4,28},{5,29},{6,30},{7,31},{8,0},{9,1},... | collective-permute-start | bytes 98312 | tf_op jit(solution)/shard_map/ppermute | solution.py:471
  93.4 1.2 %place_latents.1 = f32[32,16,128]{2,1,0:T(8,128)} custom-call(bf16[32,40,128]{2,1,0:T(8,128)(2,1)S(1)} %all-to-all-done.got), custom_call_target="tpu_custom_call" | custom-call | flops 1000000 | bytes 1048576 | tf_op jit(solution)/shard_map/place_latents/pallas_call | solution.py:380
  94.6 0.0 collective-permute-done.14.d2
  94.6 1.0 %collective-permute-done.15.d1 = bf16[1,128,128]{2,1,0:T(8,128)(2,1)S(1)} collective-permute-done((bf16[1,128,128]{2,1,0:T(8,128)(2,1)S(1)}, bf16[1,128,128]{2,1,0:T(8,128)(2,1)S(1)}, u32[]{:S(2)}, u32[]{:S(2)}) %collective-permute-start.15) | collective-permute-done | bytes 32800 | tf_op jit(solution)/shard_map/ppermute | solution.py:471
  95.6 0.0 collective-permute-done.10.e3
  95.6 0.0 collective-permute-done.11.e2
  95.6 0.0 collective-permute-done.12.e1
  95.6 0.7 sum_last_exchange.1
  (9 shorter events, 0.0 us)
Async XLA Ops:
  33.9 4.4 %collective-permute-start.4 = (bf16[256,4096]{1,0:T(8,128)(2,1)}, bf16[256,4096]{1,0:T(8,128)(2,1)S(1)}, u32[]{:S(2)}, u32[]{:S(2)}) collective-permute-start(bf16[256,4096]{1,0:T(8,128)(2,1)} %get-tuple-element.27), channel_id=1, source_target_pairs={{0,4},{1,5},{2,6},{3,7},{4,0},{5,1},{6,2},{7,3},{8,12},{9,13},{10,... | collective-permute-start | bytes 6291464 | tf_op jit(solution)/shard_map/ppermute | solution.py:423
  33.9 14.4 %collective-permute-start = (bf16[64,136,128]{2,1,0:T(8,128)(2,1)}, bf16[64,136,128]{2,1,0:T(8,128)(2,1)S(1)}, u32[]{:S(2)}, u32[]{:S(2)}) collective-permute-start(bf16[64,136,128]{2,1,0:T(8,128)(2,1)} %get-tuple-element.25), channel_id=1, source_target_pairs={{0,4},{1,5},{2,6},{3,7},{4,0},{5,1},{6,2},{7,3},{8,12},{9,13},{10,... | collective-permute-start | bytes 6684680 | tf_op jit(solution)/shard_map/ppermute | solution.py:423
  38.3 4.4 %copy-start = (bf16[960,512]{1,0:T(8,128)(2,1)S(1)}, bf16[960,512]{1,0:T(8,128)(2,1)}, u32[]{:S(2)}) copy-start(bf16[960,512]{1,0:T(8,128)(2,1)} %get-tuple-element.23.bh) | copy-start | bytes 2949124
  38.3 4.4 %copy-start.2 = (bf16[64,8,128]{2,1,0:T(8,128)(2,1)S(1)}, bf16[64,8,128]{2,1,0:T(8,128)(2,1)}, u32[]{:S(2)}) copy-start(bf16[64,8,128]{2,1,0:T(8,128)(2,1)} %get-tuple-element.24.small) | copy-start | bytes 393220
  40.6 14.9 %collective-permute-start.5 = (bf16[128,4096]{1,0:T(8,128)(2,1)S(1)}, bf16[128,4096]{1,0:T(8,128)(2,1)S(1)}, u32[]{:S(2)}, u32[]{:S(2)}) collective-permute-start(bf16[128,4096]{1,0:T(8,128)(2,1)S(1)} %get-tuple-element.52), channel_id=1, source_target_pairs={{0,1},{1,0},{2,3},{3,2},{4,7},{5,6},{6,5},{7,4},{8,9},{9,8},{10,11... | collective-permute-start | bytes 3145736 | tf_op jit(solution)/shard_map/ppermute | solution.py:454
  49.9 20.4 %collective-permute-start.1 = (bf16[16,136,128]{2,1,0:T(8,128)(2,1)S(1)}, bf16[16,136,128]{2,1,0:T(8,128)(2,1)}, u32[]{:S(2)}, u32[]{:S(2)}) collective-permute-start(bf16[16,136,128]{2,1,0:T(8,128)(2,1)S(1)} %get-tuple-element.50._), channel_id=1, source_target_pairs={{0,40},{1,41},{2,42},{3,43},{4,124},{5,125},{6,126},{7,127},{8,32}... | collective-permute-start | bytes 1671176 | tf_op jit(solution)/shard_map/ppermute | solution.py:457
  52.4 17.9 %collective-permute-start.2 = (bf16[16,136,128]{2,1,0:T(8,128)(2,1)}, bf16[16,136,128]{2,1,0:T(8,128)(2,1)}, u32[]{:S(2)}, u32[]{:S(2)}) collective-permute-start(bf16[16,136,128]{2,1,0:T(8,128)(2,1)} %get-tuple-element.49), channel_id=1, source_target_pairs={{0,32},{1,33},{2,34},{3,35},{4,100},{5,101},{6,102},{7,103},{8,40}... | collective-permute-start | bytes 1671176 | tf_op jit(solution)/shard_map/ppermute | solution.py:457
  52.9 17.4 %collective-permute-start.3 = (bf16[16,136,128]{2,1,0:T(8,128)(2,1)}, bf16[16,136,128]{2,1,0:T(8,128)(2,1)}, u32[]{:S(2)}, u32[]{:S(2)}) collective-permute-start(bf16[16,136,128]{2,1,0:T(8,128)(2,1)} %get-tuple-element.48), channel_id=1, source_target_pairs={{0,8},{1,9},{2,10},{3,11},{4,28},{5,29},{6,30},{7,31},{8,0},{9,1},... | collective-permute-start | bytes 1671176 | tf_op jit(solution)/shard_map/ppermute | solution.py:457
  55.5 5.1 %copy-start.3 = (s32[1,1,2,64]{3,2,1,0:T(2,128)S(1)}, s32[1,1,2,64]{3,2,1,0:T(2,128)}, u32[]{:S(2)}) copy-start(s32[1,1,2,64]{3,2,1,0:T(2,128)} %param.11) | copy-start | bytes 1540
  55.5 5.2 %copy-start.1 = (f32[960,128]{1,0:T(8,128)S(1)}, f32[960,128]{1,0:T(8,128)}, u32[]{:S(2)}) copy-start(f32[960,128]{1,0:T(8,128)} %get-tuple-element.31.lat) | copy-start | bytes 1474564
  56.5 13.8 %collective-permute-start.6 = (bf16[64,4096]{1,0:T(8,128)(2,1)}, bf16[64,4096]{1,0:T(8,128)(2,1)}, u32[]{:S(2)}, u32[]{:S(2)}) collective-permute-start(bf16[64,4096]{1,0:T(8,128)(2,1)} %get-tuple-element.54), channel_id=1, source_target_pairs={{0,3},{1,2},{2,1},{3,0},{4,5},{5,4},{6,7},{7,6},{8,11},{9,10},{10,... | collective-permute-start | bytes 1572872 | tf_op jit(solution)/shard_map/ppermute | solution.py:461
  62.9 16.9 %all-to-all-start = ((bf16[32,40,128]{2,1,0:T(8,128)(2,1)}), bf16[32,40,128]{2,1,0:T(8,128)(2,1)S(1)}, u32[]{:S(2)}, u32[]{:S(2)}) async-start(bf16[32,40,128]{2,1,0:T(8,128)(2,1)} %pack_latents.1), calls=%async_computation | async-start | bytes 655360 | tf_op jit(solution)/shard_map/all_to_all | solution.py:459
  72.8 10.3 %collective-permute-start.7 = (bf16[4,264,128]{2,1,0:T(8,128)(2,1)}, bf16[4,264,128]{2,1,0:T(8,128)(2,1)S(1)}, u32[]{:S(2)}, u32[]{:S(2)}) collective-permute-start(bf16[4,264,128]{2,1,0:T(8,128)(2,1)} %get-tuple-element.28), channel_id=1, source_target_pairs={{0,120},{1,121},{2,122},{3,123},{4,44},{5,45},{6,46},{7,47},{8,112... | collective-permute-start | bytes 811016 | tf_op jit(solution)/shard_map/ppermute | solution.py:464
  78.0 8.0 %collective-permute-start.8 = (bf16[4,264,128]{2,1,0:T(8,128)(2,1)}, bf16[4,264,128]{2,1,0:T(8,128)(2,1)S(1)}, u32[]{:S(2)}, u32[]{:S(2)}) collective-permute-start(bf16[4,264,128]{2,1,0:T(8,128)(2,1)} %get-tuple-element.29), channel_id=1, source_target_pairs={{0,96},{1,97},{2,98},{3,99},{4,36},{5,37},{6,38},{7,39},{8,104},{9... | collective-permute-start | bytes 811016 | tf_op jit(solution)/shard_map/ppermute | solution.py:464
  78.4 7.7 %collective-permute-start.9 = (bf16[4,264,128]{2,1,0:T(8,128)(2,1)S(1)}, bf16[4,264,128]{2,1,0:T(8,128)(2,1)S(1)}, u32[]{:S(2)}, u32[]{:S(2)}) collective-permute-start(bf16[4,264,128]{2,1,0:T(8,128)(2,1)S(1)} %get-tuple-element.30), channel_id=1, source_target_pairs={{0,24},{1,25},{2,26},{3,27},{4,12},{5,13},{6,14},{7,15},{8,16},{9,... | collective-permute-start | bytes 811016 | tf_op jit(solution)/shard_map/ppermute | solution.py:464
  86.3 5.4 %collective-permute-start.13 = (bf16[1,128,128]{2,1,0:T(8,128)(2,1)S(1)}, bf16[1,128,128]{2,1,0:T(8,128)(2,1)S(1)}, u32[]{:S(2)}, u32[]{:S(2)}) collective-permute-start(bf16[1,128,128]{2,1,0:T(8,128)(2,1)S(1)} %get-tuple-element.58), channel_id=1, source_target_pairs={{0,40},{1,41},{2,42},{3,43},{4,124},{5,125},{6,126},{7,127},{8,32}... | collective-permute-start | bytes 98312 | tf_op jit(solution)/shard_map/ppermute | solution.py:471
  86.5 9.1 %collective-permute-start.10 = (bf16[1,136,128]{2,1,0:T(8,128)(2,1)S(1)}, bf16[1,136,128]{2,1,0:T(8,128)(2,1)S(1)}, u32[]{:S(2)}, u32[]{:S(2)}) collective-permute-start(bf16[1,136,128]{2,1,0:T(8,128)(2,1)S(1)} %get-tuple-element.61), channel_id=1, source_target_pairs={{0,2},{1,3},{2,0},{3,1},{4,6},{5,7},{6,4},{7,5},{8,10},{9,11},{10,... | collective-permute-start | bytes 104456 | tf_op jit(solution)/shard_map/ppermute | solution.py:470
  88.0 7.6 %collective-permute-start.11 = (bf16[1,136,128]{2,1,0:T(8,128)(2,1)S(1)}, bf16[1,136,128]{2,1,0:T(8,128)(2,1)S(1)}, u32[]{:S(2)}, u32[]{:S(2)}) collective-permute-start(bf16[1,136,128]{2,1,0:T(8,128)(2,1)S(1)} %get-tuple-element.60), channel_id=1, source_target_pairs={{0,3},{1,0},{2,1},{3,2},{4,7},{5,4},{6,5},{7,6},{8,11},{9,8},{10,9... | collective-permute-start | bytes 104456 | tf_op jit(solution)/shard_map/ppermute | solution.py:470
  89.2 6.5 %collective-permute-start.12 = (bf16[1,136,128]{2,1,0:T(8,128)(2,1)S(1)}, bf16[1,136,128]{2,1,0:T(8,128)(2,1)S(1)}, u32[]{:S(2)}, u32[]{:S(2)}) collective-permute-start(bf16[1,136,128]{2,1,0:T(8,128)(2,1)S(1)} %get-tuple-element.59), channel_id=1, source_target_pairs={{0,1},{1,2},{2,3},{3,0},{4,5},{5,6},{6,7},{7,4},{8,9},{9,10},{10,1... | collective-permute-start | bytes 104456 | tf_op jit(solution)/shard_map/ppermute | solution.py:470
  90.0 4.5 %collective-permute-start.14 = (bf16[1,128,128]{2,1,0:T(8,128)(2,1)S(1)}, bf16[1,128,128]{2,1,0:T(8,128)(2,1)S(1)}, u32[]{:S(2)}, u32[]{:S(2)}) collective-permute-start(bf16[1,128,128]{2,1,0:T(8,128)(2,1)S(1)} %get-tuple-element.57), channel_id=1, source_target_pairs={{0,32},{1,33},{2,34},{3,35},{4,100},{5,101},{6,102},{7,103},{8,40}... | collective-permute-start | bytes 98312 | tf_op jit(solution)/shard_map/ppermute | solution.py:471
  91.7 3.9 %collective-permute-start.15 = (bf16[1,128,128]{2,1,0:T(8,128)(2,1)S(1)}, bf16[1,128,128]{2,1,0:T(8,128)(2,1)S(1)}, u32[]{:S(2)}, u32[]{:S(2)}) collective-permute-start(bf16[1,128,128]{2,1,0:T(8,128)(2,1)S(1)} %get-tuple-element.56), channel_id=1, source_target_pairs={{0,8},{1,9},{2,10},{3,11},{4,28},{5,29},{6,30},{7,31},{8,0},{9,1},... | collective-permute-start | bytes 98312 | tf_op jit(solution)/shard_map/ppermute | solution.py:471
